TPU v7x, 32 devices: a whole 2x2x4 slice. The times are simulated.
32 devices in a mesh: batch: 2 (over x), frame: 4 (over z), tensor: 4 (over y, core).
Axes of the slice: x: 2, y: 2, z: 4, core: 2. Of those that a mesh axis runs over, the one named last changes fastest.
Arguments:
- tokens: bfloat16 [16, 4, 256, 1024], P('batch', 'frame', 'tensor'), may hold values from -6 to 6
- noise_level: float32 [16, 4], P('batch', 'frame'), may hold values from 0 to 1
- w_ada: bfloat16 [1024, 6, 1024], P(None, None, 'tensor'), may hold values from -0.375 to 0.375
- b_ada: bfloat16 [6, 1024], P(None, 'tensor'), may hold values from -1.75 to 1.75
- w_qkv: bfloat16 [1024, 3, 1024], P(None, None, 'tensor'), may hold values from -0.1875 to 0.1875
- b_qkv: bfloat16 [3, 1024], P(None, 'tensor'), may hold values from -1.75 to 1.75
- w_out: bfloat16 [1024, 1024], P('tensor'), may hold values from -0.75 to 0.75
- b_out: bfloat16 [1024], replicated, may hold values from -1.75 to 1.75
- w_fc1: bfloat16 [1024, 4096], P(None, 'tensor'), may hold values from -0.1875 to 0.1875
- b_fc1: bfloat16 [4096], P('tensor'), may hold values from -1.75 to 1.75
- w_fc2: bfloat16 [4096, 1024], P('tensor'), may hold values from -0.09375 to 0.09375
- b_fc2: bfloat16 [1024], replicated, may hold values from -1.75 to 1.75
- cotangent: bfloat16 [16, 4, 256, 1024], P('batch', 'frame', 'tensor'), may hold values from -6 to 6
Outputs:
- output: bfloat16 [16, 4, 256, 1024], P('batch', 'frame', 'tensor')
- tokens_grad: float32 [16, 4, 256, 1024], P('batch', 'frame', 'tensor')
- ada_grad: float32 [1024, 6, 1024], P(None, None, 'tensor')
- ada_bias_grad: float32 [6, 1024], P(None, 'tensor')
- qkv_grad: float32 [1024, 3, 1024], P(None, None, 'tensor')
- qkv_bias_grad: float32 [3, 1024], P(None, 'tensor')
- out_grad: float32 [1024, 1024], P('tensor')
- out_bias_grad: float32 [1024], replicated
- fc1_grad: float32 [1024, 4096], P(None, 'tensor')
- fc1_bias_grad: float32 [4096], P('tensor')
- fc2_grad: float32 [4096, 1024], P('tensor')
- fc2_bias_grad: float32 [1024], replicated
All inputs are finite; a program needn't handle non-finite values.
Results may differ from a plain program's by a relative error of at most 0.019.
The roundings to bfloat16 on the way count: a program that leaves them out, or rounds other values in their place, can miss the bound.
Values may be sent and summed in bfloat16 or wider, within the bound.
A program may use at most 256 MiB of HBM per device.

v0:
```python
from functools import partial
import math

import jax
import jax.numpy as jnp
from jax import lax
from jax.sharding import PartitionSpec as P

HD = 64
GRID = 16
PATCHES = 256


epsilon = 1e-06


def frequencies(count):
    return 10000.0 ** (-(jnp.arange(count, dtype=jnp.float32) / count))


def rotate_half(segment, position):
    half = segment.shape[-1] // 2
    angle = position[..., None] * frequencies(half)
    cosine = jnp.cos(angle)
    sine = jnp.sin(angle)
    first = segment[..., :half]
    second = segment[..., half:]
    return jnp.concatenate(
        [first * cosine - second * sine, first * sine + second * cosine], axis=-1
    )


def rotary(vector, frame_pos, row_pos, col_pos):
    width = vector.shape[-1]
    first = width // 4
    middle = (width - first) // 2
    return jnp.concatenate(
        [
            rotate_half(vector[..., :first], frame_pos),
            rotate_half(vector[..., first : first + middle], row_pos),
            rotate_half(vector[..., first + middle :], col_pos),
        ],
        axis=-1,
    )


def embedding(level, width):
    half = width // 2
    angle = 1000.0 * level[..., None] * frequencies(half)
    return jnp.concatenate([jnp.cos(angle), jnp.sin(angle)], axis=-1)


def normalize(value):
    center = value - jnp.mean(value, axis=-1, keepdims=True)
    spread = jnp.mean(center * center, axis=-1, keepdims=True)
    return center * lax.rsqrt(spread + epsilon)


def modulate(value, shift, scale):
    return normalize(value) * (1.0 + scale) + shift


def body(
    tokens,
    noise_level,
    w_ada,
    b_ada,
    w_qkv,
    b_qkv,
    w_out,
    b_out,
    w_fc1,
    b_fc1,
    w_fc2,
    b_fc2,
    cotangent,
):
    clips = tokens.shape[0]
    width = tokens.shape[3]
    head_cols = w_qkv.shape[2]
    heads_here = head_cols // HD
    frames = lax.axis_size("frame")
    frame_now = lax.axis_index("frame")
    scale = 1.0 / math.sqrt(HD)
    condition = jax.nn.silu(embedding(noise_level, width)).astype(jnp.bfloat16)
    mod_part = jnp.einsum(
        "cfd,dke->cfke", condition, w_ada, preferred_element_type=jnp.float32
    ) + b_ada.astype(jnp.float32)
    modulation = lax.all_gather(mod_part, "tensor", axis=3, tiled=True)
    pieces = [modulation[:, :, slot : slot + 1, :] for slot in range(6)]
    resid_in = tokens.astype(jnp.float32)
    attn_val, ln_one_back = jax.vjp(modulate, resid_in, pieces[0], pieces[1])
    attn_rows = lax.all_gather(attn_val.astype(jnp.bfloat16), "tensor", axis=2, tiled=True)
    projected = jnp.einsum(
        "cfpd,dke->cfpke", attn_rows, w_qkv, preferred_element_type=jnp.float32
    ) + b_qkv.astype(jnp.float32)
    projected = projected[:, 0]
    patch_ids = jnp.arange(PATCHES)
    row_pos = (patch_ids // GRID).astype(jnp.float32)[:, None]
    col_pos = (patch_ids % GRID).astype(jnp.float32)[:, None]
    frame_pos = frame_now.astype(jnp.float32)

    def turned(vector):
        return rotary(vector.reshape(clips, PATCHES, heads_here, HD), frame_pos, row_pos, col_pos)

    query_rot, query_back = jax.vjp(turned, projected[:, :, 0])
    key_rot, key_back = jax.vjp(turned, projected[:, :, 1])
    queries = query_rot.astype(jnp.bfloat16).reshape(clips, PATCHES, head_cols)
    keys_here = key_rot.astype(jnp.bfloat16).reshape(clips, PATCHES, head_cols)
    values_here = projected[:, :, 2].astype(jnp.bfloat16)
    kv_own = jnp.concatenate([keys_here, values_here], axis=-1)[:, None]
    allowed = jnp.arange(frames * PATCHES) // PATCHES <= frame_now
    kv_all = lax.all_gather(kv_own, "frame", axis=1, tiled=True)

    def fetch(index):
        return lax.dynamic_index_in_dim(kv_all, index, 0, False)

    def score_block(query_clip, kv_clip):
        keys = kv_clip[..., :head_cols].reshape(frames * PATCHES, heads_here, HD)
        values = kv_clip[..., head_cols:].reshape(frames * PATCHES, heads_here, HD)
        scores = (
            jnp.einsum(
                "qhd,khd->hqk",
                query_clip.reshape(PATCHES, heads_here, HD),
                keys,
                preferred_element_type=jnp.float32,
            )
            * scale
        )
        return (jnp.where(allowed[None, None, :], scores, -1e30), keys, values)

    def forward_step(carry, index):
        query_clip = lax.dynamic_index_in_dim(queries, index, 0, False)
        scores, keys, values = score_block(query_clip, fetch(index))
        row_max = jnp.max(scores, axis=-1, keepdims=True)
        exp_scores = jnp.exp(scores - row_max)
        row_sum = jnp.sum(exp_scores, axis=-1, keepdims=True)
        prob_map = exp_scores / row_sum
        mixed = jnp.einsum(
            "hqk,khd->qhd",
            prob_map.astype(jnp.bfloat16),
            values,
            preferred_element_type=jnp.float32,
        ).reshape(PATCHES, head_cols)
        return (carry, (mixed, (row_max + jnp.log(row_sum))[..., 0]))

    _, (mixed_all, log_sums) = lax.scan(forward_step, None, jnp.arange(clips))
    mixed_low = mixed_all.astype(jnp.bfloat16)
    attn_term = jnp.einsum("cpj,jd->cpd", mixed_low, w_out, preferred_element_type=jnp.float32)[
        :, None
    ]
    attn_branch = lax.psum_scatter(
        attn_term, "tensor", scatter_dimension=2, tiled=True
    ) + b_out.astype(jnp.float32)
    resid_one = resid_in + pieces[2] * attn_branch
    mlp_val, ln_two_back = jax.vjp(modulate, resid_one, pieces[3], pieces[4])
    mlp_rows = lax.all_gather(mlp_val.astype(jnp.bfloat16), "tensor", axis=2, tiled=True)
    pre_act = jnp.einsum(
        "cfpd,dj->cfpj", mlp_rows, w_fc1, preferred_element_type=jnp.float32
    ) + b_fc1.astype(jnp.float32)
    act_val, gelu_back = jax.vjp(partial(jax.nn.gelu, approximate=True), pre_act)
    activated = act_val.astype(jnp.bfloat16)
    mlp_term = jnp.einsum("cfpj,jd->cfpd", activated, w_fc2, preferred_element_type=jnp.float32)
    mlp_branch = lax.psum_scatter(
        mlp_term, "tensor", scatter_dimension=2, tiled=True
    ) + b_fc2.astype(jnp.float32)
    output = (resid_one + pieces[5] * mlp_branch).astype(jnp.bfloat16)
    upstream = cotangent.astype(jnp.float32)
    mlp_grad = (pieces[5] * upstream).astype(jnp.bfloat16)
    gate_two_grad = jnp.sum(upstream * mlp_branch, axis=2, keepdims=True)
    mlp_grad_rows = lax.all_gather(mlp_grad, "tensor", axis=2, tiled=True)
    fc2_grad = jnp.einsum(
        "cfpj,cfpd->jd", activated, mlp_grad_rows, preferred_element_type=jnp.float32
    )
    fc2_bias_grad = jnp.sum(mlp_grad_rows.astype(jnp.float32), axis=(0, 1, 2))
    act_grad = jnp.einsum("cfpd,jd->cfpj", mlp_grad_rows, w_fc2, preferred_element_type=jnp.float32)
    pre_grad = gelu_back(act_grad)[0].astype(jnp.bfloat16)
    fc1_grad = jnp.einsum("cfpd,cfpj->dj", mlp_rows, pre_grad, preferred_element_type=jnp.float32)
    fc1_bias_grad = jnp.sum(pre_grad.astype(jnp.float32), axis=(0, 1, 2))
    mlp_in_term = jnp.einsum("cfpj,dj->cfpd", pre_grad, w_fc1, preferred_element_type=jnp.float32)
    mlp_in_grad = lax.psum_scatter(mlp_in_term, "tensor", scatter_dimension=2, tiled=True)
    resid_part, shift_two_grad, scale_two_grad = ln_two_back(mlp_in_grad)
    resid_grad = upstream + resid_part
    attn_grad = (pieces[2] * resid_grad).astype(jnp.bfloat16)
    gate_one_grad = jnp.sum(resid_grad * attn_branch, axis=2, keepdims=True)
    attn_grad_rows = lax.all_gather(attn_grad, "tensor", axis=2, tiled=True)[:, 0]
    out_grad = jnp.einsum(
        "cpj,cpd->jd", mixed_low, attn_grad_rows, preferred_element_type=jnp.float32
    )
    out_bias_grad = jnp.sum(attn_grad_rows.astype(jnp.float32), axis=(0, 1))
    mixed_grad = jnp.einsum(
        "cpd,jd->cpj", attn_grad_rows, w_out, preferred_element_type=jnp.float32
    ).astype(jnp.bfloat16)

    def query_side(index):
        query_clip = lax.dynamic_index_in_dim(queries, index, 0, False)
        grad_clip = lax.dynamic_index_in_dim(mixed_grad, index, 0, False)
        lse_clip = lax.dynamic_index_in_dim(log_sums, index, 0, False)
        scores, keys, values = score_block(query_clip, fetch(index))
        prob_map = jnp.exp(scores - lse_clip[..., None])
        grad_heads = grad_clip.reshape(PATCHES, heads_here, HD)
        prob_grad = jnp.einsum(
            "qhd,khd->hqk", grad_heads, values, preferred_element_type=jnp.float32
        )
        row_dot = jnp.sum(prob_map * prob_grad, axis=-1, keepdims=True)
        score_grad = (scale * prob_map * (prob_grad - row_dot)).astype(jnp.bfloat16)
        query_grad = jnp.einsum(
            "hqk,khd->qhd", score_grad, keys, preferred_element_type=jnp.float32
        ).reshape(PATCHES, head_cols)
        return (query_clip, grad_heads, prob_map, score_grad, row_dot, query_grad)

    def backward_step(carry, index):
        query_clip, grad_heads, prob_map, score_grad, row_dot, query_grad = query_side(index)
        key_grad = jnp.einsum(
            "hqk,qhd->khd",
            score_grad,
            query_clip.reshape(PATCHES, heads_here, HD),
            preferred_element_type=jnp.float32,
        ).reshape(frames, PATCHES, head_cols)
        value_grad = jnp.einsum(
            "hqk,qhd->khd",
            prob_map.astype(jnp.bfloat16),
            grad_heads,
            preferred_element_type=jnp.float32,
        ).reshape(frames, PATCHES, head_cols)
        owned = lax.psum_scatter(
            jnp.concatenate([key_grad, value_grad], axis=-1),
            "frame",
            scatter_dimension=0,
            tiled=True,
        )
        return (carry, (query_grad, owned[0]))

    _, (query_grads, kv_grads) = lax.scan(backward_step, None, jnp.arange(clips))
    query_raw_grad = query_back(query_grads.reshape(clips, PATCHES, heads_here, HD))[0]
    key_raw_grad = key_back(kv_grads[..., :head_cols].reshape(clips, PATCHES, heads_here, HD))[0]
    projected_grad = jnp.stack([query_raw_grad, key_raw_grad, kv_grads[..., head_cols:]], axis=2)
    projected_grad = projected_grad.astype(jnp.bfloat16)[:, None]
    qkv_grad = jnp.einsum(
        "cfpd,cfpke->dke", attn_rows, projected_grad, preferred_element_type=jnp.float32
    )
    qkv_bias_grad = jnp.sum(projected_grad.astype(jnp.float32), axis=(0, 1, 2))
    attn_in_term = jnp.einsum(
        "cfpke,dke->cfpd", projected_grad, w_qkv, preferred_element_type=jnp.float32
    )
    attn_in_grad = lax.psum_scatter(attn_in_term, "tensor", scatter_dimension=2, tiled=True)
    input_part, shift_one_grad, scale_one_grad = ln_one_back(attn_in_grad)
    tokens_grad = resid_grad + input_part
    mod_grad_part = jnp.concatenate(
        [
            shift_one_grad,
            scale_one_grad,
            gate_one_grad,
            shift_two_grad,
            scale_two_grad,
            gate_two_grad,
        ],
        axis=2,
    )
    mod_grad = lax.psum_scatter(mod_grad_part, "tensor", scatter_dimension=3, tiled=True)
    ada_grad = jnp.einsum(
        "cfd,cfke->dke", condition.astype(jnp.float32), mod_grad, precision=lax.Precision.HIGHEST
    )
    ada_bias_grad = jnp.sum(mod_grad, axis=(0, 1))
    summed = lax.psum(
        (
            ada_grad,
            ada_bias_grad,
            qkv_grad,
            qkv_bias_grad,
            out_grad,
            out_bias_grad,
            fc1_grad,
            fc1_bias_grad,
            fc2_grad,
            fc2_bias_grad,
        ),
        ("batch", "frame"),
    )
    return (
        output,
        tokens_grad,
        summed[0],
        summed[1],
        summed[2],
        summed[3],
        summed[4],
        summed[5],
        summed[6],
        summed[7],
        summed[8],
        summed[9],
    )


def solution(mesh):
    return jax.shard_map(
        body,
        mesh=mesh,
        in_specs=(
            P("batch", "frame", "tensor", None),
            P("batch", "frame"),
            P(None, None, "tensor"),
            P(None, "tensor"),
            P(None, None, "tensor"),
            P(None, "tensor"),
            P("tensor", None),
            P(),
            P(None, "tensor"),
            P("tensor"),
            P("tensor", None),
            P(),
            P("batch", "frame", "tensor", None),
        ),
        out_specs=(
            P("batch", "frame", "tensor", None),
            P("batch", "frame", "tensor", None),
            P(None, None, "tensor"),
            P(None, "tensor"),
            P(None, None, "tensor"),
            P(None, "tensor"),
            P("tensor", None),
            P(),
            P(None, "tensor"),
            P("tensor"),
            P("tensor", None),
            P(),
        ),
        check_vma=False,
    )
```

profile of v0, /device:TPU:0, one launch (start us, length us, event | category | flops | bytes accessed | tf_op | source)
XLA Modules:
  0.0 2032.3 jit_solution(12831585807642381794)
XLA Ops:
  13.0 7.0 all-gather
  22.6 35.7 %all-gather.8.cloned.1.call-done = bf16[8,1,256,1024]{3,2,0,1:T(8,128)(2,1)} async-done(((bf16[8,1,64,1024]{3,2,0,1:T(8,128)(2,1)}), bf16[8,1,256,1024]{3,2,0,1:T(8,128)(2,1)}) %all-gather.8.cloned.1.call-update) | async-done | bytes 4194320 | tf_op jit(solution)/shard_map/all_gather | solution.py:93
  66.5 14.0 concatenate.41
  84.9 10.3 concatenate.43
  95.2 137.2 %all-gather.16.cloned.1.call-done = bf16[8,1024,512]{1,2,0:T(8,128)(2,1)} async-done(((bf16[8,256,512]{1,2,0:T(8,128)(2,1)}), bf16[8,1024,512]{1,2,0:T(8,128)(2,1)}) %all-gather.16.cloned.1.call-update) | async-done | bytes 8388624 | tf_op jit(solution)/shard_map/all_gather | solution.py:113
  232.5 14.5 reshape.658
  247.0 86.0 %while.28 = (s32[]{:T(128)}, bf16[8,256,256]{1,2,0:T(8,128)(2,1)}, f32[8,4,256]{2,1,0:T(4,128)}, s32[8]{0:T(128)S(1)}, bf16[8,4,256,512]{2,1,3,0:T(4,128)(2,1)}, /*index=5*/bf16[8,256,256]{1,2,0:T(8,128)(2,1)}, s32[]{:T(128)}) while((s32[]{:T(128)}, bf16[8,256,256]{1,2,0:T(8,128)(2,1)}, f32[8,4,256]{2,1,0:T(4,128)}, ...), condition=%wide.region_5.6_spmd.clone.clone, body=%wide.region_2.5_spmd.clone.sunk.clone | while | flops 281026560 | bytes 20746392 | solution.py:147
  339.5 69.4 %reduce-scatter.7.cloned.1.call-done = f32[8,1,64,1024]{3,2,0,1:T(8,128)} async-done(((f32[8,1,256,1024]{3,2,0,1:T(8,128)}), f32[8,1,64,1024]{3,2,0,1:T(8,128)}) %reduce-scatter.7.cloned.1.call-update) | async-done | bytes 2097168 | tf_op jit(solution)/shard_map/reduce_scatter | solution.py:152
  414.8 32.6 %all-gather.10.cloned.1.call-done = bf16[8,1,256,1024]{3,2,0,1:T(8,128)(2,1)} async-done(((bf16[8,1,64,1024]{3,2,0,1:T(8,128)(2,1)}), bf16[8,1,256,1024]{3,2,0,1:T(8,128)(2,1)}) %all-gather.10.cloned.1.call-update) | async-done | bytes 4194320 | tf_op jit(solution)/shard_map/all_gather | solution.py:157
  447.4 11.4 fusion.46
  458.8 25.2 %all-gather.12.cloned.1.call-done = bf16[8,1,256,1024]{3,2,0,1:T(8,128)(2,1)} async-done(((bf16[8,1,64,1024]{3,2,0,1:T(8,128)(2,1)}), bf16[8,1,256,1024]{3,2,0,1:T(8,128)(2,1)}) %all-gather.12.cloned.1.call-update) | async-done | bytes 4194320 | tf_op jit(solution)/shard_map/all_gather | solution.py:171
  484.0 13.8 convert_reduce_fusion.1
  507.0 71.6 %reduce-scatter.11.cloned.1.call-done = f32[8,1,64,1024]{3,2,0,1:T(8,128)} async-done(((f32[8,1,256,1024]{3,2,0,1:T(8,128)}), f32[8,1,64,1024]{3,2,0,1:T(8,128)}) %reduce-scatter.11.cloned.1.call-update) | async-done | bytes 2097168 | tf_op jit(solution)/shard_map/reduce_scatter | solution.py:181
  585.4 34.6 %all-gather.14.cloned.1.call-done = bf16[8,1,256,1024]{3,2,0,1:T(8,128)(2,1)} async-done(((bf16[8,1,64,1024]{3,2,0,1:T(8,128)(2,1)}), bf16[8,1,256,1024]{3,2,0,1:T(8,128)(2,1)}) %all-gather.14.cloned.1.call-update) | async-done | bytes 4194320 | tf_op jit(solution)/shard_map/all_gather | solution.py:186
  624.5 607.9 %while.29 = (s32[]{:T(128)}, f32[8,256,256]{1,2,0:T(8,128)}, f32[8,256,512]{2,1,0:T(8,128)}, s32[8]{0:T(128)S(1)}, bf16[8,4,256,512]{2,1,3,0:T(4,128)(2,1)}, /*i...) while((s32[]{:T(128)}, f32[8,256,256]{1,2,0:T(8,128)}, ...), condition=%wide.region_16.17_spmd.clone.clone, body=%wide.region_13.16_spmd.clone.sunk.clone | while | flops 688398336 | bytes 98599184 | solution.py:234
  656.7 42.5 %reduce-scatter.17.cloned.1.call-done = f32[1,256,512]{2,1,0:T(8,128)} async-done(((f32[4,256,512]{2,1,0:T(8,128)}), f32[1,256,512]{2,1,0:T(8,128)}) %reduce-scatter.17.cloned.1.call-update) | async-done | bytes 524304 | tf_op jit(solution)/shard_map/while/body/eval_jaxpr/reduce_scatter | solution.py:226
  733.3 41.9 %reduce-scatter.17.cloned.1.call-done = f32[1,256,512]{2,1,0:T(8,128)} async-done(((f32[4,256,512]{2,1,0:T(8,128)}), f32[1,256,512]{2,1,0:T(8,128)}) %reduce-scatter.17.cloned.1.call-update) | async-done | bytes 524304 | tf_op jit(solution)/shard_map/while/body/eval_jaxpr/reduce_scatter | solution.py:226
  809.2 41.8 %reduce-scatter.17.cloned.1.call-done = f32[1,256,512]{2,1,0:T(8,128)} async-done(((f32[4,256,512]{2,1,0:T(8,128)}), f32[1,256,512]{2,1,0:T(8,128)}) %reduce-scatter.17.cloned.1.call-update) | async-done | bytes 524304 | tf_op jit(solution)/shard_map/while/body/eval_jaxpr/reduce_scatter | solution.py:226
  885.1 41.9 %reduce-scatter.17.cloned.1.call-done = f32[1,256,512]{2,1,0:T(8,128)} async-done(((f32[4,256,512]{2,1,0:T(8,128)}), f32[1,256,512]{2,1,0:T(8,128)}) %reduce-scatter.17.cloned.1.call-update) | async-done | bytes 524304 | tf_op jit(solution)/shard_map/while/body/eval_jaxpr/reduce_scatter | solution.py:226
  961.0 41.9 %reduce-scatter.17.cloned.1.call-done = f32[1,256,512]{2,1,0:T(8,128)} async-done(((f32[4,256,512]{2,1,0:T(8,128)}), f32[1,256,512]{2,1,0:T(8,128)}) %reduce-scatter.17.cloned.1.call-update) | async-done | bytes 524304 | tf_op jit(solution)/shard_map/while/body/eval_jaxpr/reduce_scatter | solution.py:226
  1036.9 41.9 %reduce-scatter.17.cloned.1.call-done = f32[1,256,512]{2,1,0:T(8,128)} async-done(((f32[4,256,512]{2,1,0:T(8,128)}), f32[1,256,512]{2,1,0:T(8,128)}) %reduce-scatter.17.cloned.1.call-update) | async-done | bytes 524304 | tf_op jit(solution)/shard_map/while/body/eval_jaxpr/reduce_scatter | solution.py:226
  1112.8 41.9 %reduce-scatter.17.cloned.1.call-done = f32[1,256,512]{2,1,0:T(8,128)} async-done(((f32[4,256,512]{2,1,0:T(8,128)}), f32[1,256,512]{2,1,0:T(8,128)}) %reduce-scatter.17.cloned.1.call-update) | async-done | bytes 524304 | tf_op jit(solution)/shard_map/while/body/eval_jaxpr/reduce_scatter | solution.py:226
  1188.7 41.8 %reduce-scatter.17.cloned.1.call-done = f32[1,256,512]{2,1,0:T(8,128)} async-done(((f32[4,256,512]{2,1,0:T(8,128)}), f32[1,256,512]{2,1,0:T(8,128)}) %reduce-scatter.17.cloned.1.call-update) | async-done | bytes 524304 | tf_op jit(solution)/shard_map/while/body/eval_jaxpr/reduce_scatter | solution.py:226
  1248.3 9.2 convolution_bitcast_fusion.4
  1259.1 13.3 convolution_bitcast_fusion.2
  1273.1 10.2 fusion.56
  1283.3 11.6 fusion.59
  1300.5 28.2 %reduce-scatter.13.cloned.1.call-done = f32[8,1,64,1024]{3,2,0,1:T(8,128)} async-done(((f32[8,1,256,1024]{3,2,0,1:T(8,128)}), f32[8,1,64,1024]{3,2,0,1:T(8,128)}) %reduce-scatter.13.cloned.1.call-update) | async-done | bytes 2097168 | tf_op jit(solution)/shard_map/reduce_scatter | solution.py:246
  1333.6 69.4 %reduce-scatter.9.cloned.1.call-done = f32[8,1,64,1024]{3,2,0,1:T(8,128)} async-done(((f32[8,1,256,1024]{3,2,0,1:T(8,128)}), f32[8,1,64,1024]{3,2,0,1:T(8,128)}) %reduce-scatter.9.cloned.1.call-update) | async-done | bytes 2097168 | tf_op jit(solution)/shard_map/reduce_scatter | solution.py:164
  1414.5 15.1 reduce-scatter.15.cloned.1.call-done
  1444.7 40.5 %all-reduce.18 = (f32[6,256]{1,0:T(8,128)}, f32[3,256]{1,0:T(4,128)}, f32[1024]{0:T(1024)}, f32[1024]{0:T(1024)}, f32[1024]{0:T(1024)}) all-reduce(f32[6,256]{1,0:T(8,128)S(1)} %reduce_sum.219, f32[3,256]{1,0:T(4,128)S(1)} %convert_reduce_fusion.3, ...), channel_id=1, replica_groups=mesh['batch'=2,'frame'=4,'tensor'=4] {'batch','frame'}, use_global_device_ids=true, to_apply=%region_29.30 | all-reduce | flops 5376 | bytes 43008 | tf_op jit(solution)/shard_map/psum | solution.py:265
  1485.2 524.1 %all-reduce.22.cloned.1.call-done = (f32[1024,6,256]{2,0,1:T(8,128)}, f32[1024,3,256]{2,0,1:T(8,128)}, f32[256,1024]{1,0:T(8,128)}, f32[1024,1024]{1,0:T(8,128)}, f32[1024,1024]{1,0:T(8,128)}) async-done(((f32[1024,6,256]{2,0,1:T(8,128)}, f32[1024,3,256]{2,0,1:T(8,128)}, f32[256,1024]{1,0:T(8,128)}, f32[1024,1024]{1,0:T(8,128)}, f32[1024,1024]{1,0:T(8,128)}), (f32[1024,6,256]{2,0,1:T(8,128)}, ...) | async-done | bytes 18874384 | tf_op jit(solution)/shard_map/psum | solution.py:265
  (589 shorter events, 450.7 us)
Async XLA Ops:
  7.2 51.1 %all-gather.8.cloned.1.call-start = ((), (), s32[]{:S(2)}) async-start(), calls=%async_computation.6 | async-start | bytes 5242880 | tf_op jit(solution)/shard_map/all_gather | solution.py:93
  20.6 392.2 %copy-start.44 = (f32[8,1024]{1,0:T(8,128)}, f32[8,1024]{1,0:T(8,128)S(1)}, u32[]{:S(2)}) copy-start(f32[8,1024]{1,0:T(8,128)S(1)} %get-tuple-element.303) | copy-start | bytes 98308
  22.2 210.3 %all-gather.16.cloned.1.call-start = ((), (), s32[]{:S(2)}) async-start(), calls=%async_computation.15 | async-start | bytes 10485760 | tf_op jit(solution)/shard_map/all_gather | solution.py:113
  22.6 62.0 %copy-start.36 = (f32[256,12]{0,1:T(8,128)}, f32[256,12]{0,1:T(8,128)S(1)}, u32[]{:S(2)}) copy-start(f32[256,12]{0,1:T(8,128)S(1)} %get-tuple-element.311) | copy-start | bytes 36868
  22.6 62.0 %copy-start.38 = (f32[256,12]{0,1:T(8,128)}, f32[256,12]{0,1:T(8,128)S(1)}, u32[]{:S(2)}) copy-start(f32[256,12]{0,1:T(8,128)S(1)} %get-tuple-element.312) | copy-start | bytes 36868
  83.2 325.7 %reduce-scatter.7.cloned.1.call-start = ((), (), s32[]{:S(2)}) async-start(), calls=%async_computation.7 | async-start | bytes 10485760 | tf_op jit(solution)/shard_map/reduce_scatter | solution.py:152
  247.0 86.0 %copy-start.32 = (bf16[256,1024]{1,0:T(8,128)(2,1)S(1)}, bf16[256,1024]{1,0:T(8,128)(2,1)}, u32[]{:S(2)}) copy-start(bf16[256,1024]{1,0:T(8,128)(2,1)} %param.23) | copy-start | bytes 1572868
  338.8 70.1 %copy-start.7 = (bf16[8,1,64,1024]{3,2,1,0:T(8,128)(2,1)S(1)}, bf16[8,1,64,1024]{3,2,1,0:T(8,128)(2,1)}, u32[]{:S(2)}) copy-start(bf16[8,1,64,1024]{3,2,1,0:T(8,128)(2,1)} %param.17) | copy-start | bytes 3145732
  338.8 70.1 %copy-start.46 = (f32[8,1024]{1,0:T(8,128)S(1)}, f32[8,1024]{1,0:T(8,128)}, u32[]{:S(2)}) copy-start(f32[8,1024]{1,0:T(8,128)} %get-tuple-element.308) | copy-start | bytes 98308
  338.8 108.6 %all-gather.10.cloned.1.call-start = ((), (), s32[]{:S(2)}) async-start(), calls=%async_computation.8 | async-start | bytes 5242880 | tf_op jit(solution)/shard_map/all_gather | solution.py:157
  339.5 71.4 %copy-start.60 = (f32[1024]{0:T(1024)}, f32[1024]{0:T(1024)S(1)}, u32[]{:S(2)}) copy-start(f32[1024]{0:T(1024)S(1)} %convert_element_type.202) | copy-start | bytes 12292
  410.9 171.0 %copy-start.4 = (f32[8,1,64,1024]{3,2,0,1:T(8,128)}, f32[8,1,64,1024]{3,2,0,1:T(8,128)S(1)}, u32[]{:S(2)}) copy-start(f32[8,1,64,1024]{3,2,0,1:T(8,128)S(1)} %get-tuple-element.256) | copy-start | bytes 6291460
  412.8 71.2 %all-gather.12.cloned.1.call-start = ((), (), s32[]{:S(2)}) async-start(), calls=%async_computation.10 | async-start | bytes 5242880 | tf_op jit(solution)/shard_map/all_gather | solution.py:171
  414.2 164.4 %reduce-scatter.11.cloned.1.call-start = ((), (), s32[]{:S(2)}) async-start(), calls=%async_computation.11 | async-start | bytes 10485760 | tf_op jit(solution)/shard_map/reduce_scatter | solution.py:181
  506.8 113.2 %all-gather.14.cloned.1.call-start = ((), (), s32[]{:S(2)}) async-start(), calls=%async_computation.12 | async-start | bytes 5242880 | tf_op jit(solution)/shard_map/all_gather | solution.py:186
  624.5 74.7 %reduce-scatter.17.cloned.1.call-start = ((), (), s32[]{:S(2)}) async-start(), calls=%async_computation.17 | async-start | bytes 2621440 | tf_op jit(solution)/shard_map/while/body/eval_jaxpr/reduce_scatter | solution.py:226
  701.1 74.0 %reduce-scatter.17.cloned.1.call-start = ((), (), s32[]{:S(2)}) async-start(), calls=%async_computation.17 | async-start | bytes 2621440 | tf_op jit(solution)/shard_map/while/body/eval_jaxpr/reduce_scatter | solution.py:226
  777.0 74.0 %reduce-scatter.17.cloned.1.call-start = ((), (), s32[]{:S(2)}) async-start(), calls=%async_computation.17 | async-start | bytes 2621440 | tf_op jit(solution)/shard_map/while/body/eval_jaxpr/reduce_scatter | solution.py:226
  852.9 74.0 %reduce-scatter.17.cloned.1.call-start = ((), (), s32[]{:S(2)}) async-start(), calls=%async_computation.17 | async-start | bytes 2621440 | tf_op jit(solution)/shard_map/while/body/eval_jaxpr/reduce_scatter | solution.py:226
  928.8 74.0 %reduce-scatter.17.cloned.1.call-start = ((), (), s32[]{:S(2)}) async-start(), calls=%async_computation.17 | async-start | bytes 2621440 | tf_op jit(solution)/shard_map/while/body/eval_jaxpr/reduce_scatter | solution.py:226
  1004.7 74.0 %reduce-scatter.17.cloned.1.call-start = ((), (), s32[]{:S(2)}) async-start(), calls=%async_computation.17 | async-start | bytes 2621440 | tf_op jit(solution)/shard_map/while/body/eval_jaxpr/reduce_scatter | solution.py:226
  1080.6 74.0 %reduce-scatter.17.cloned.1.call-start = ((), (), s32[]{:S(2)}) async-start(), calls=%async_computation.17 | async-start | bytes 2621440 | tf_op jit(solution)/shard_map/while/body/eval_jaxpr/reduce_scatter | solution.py:226
  1156.5 74.0 %reduce-scatter.17.cloned.1.call-start = ((), (), s32[]{:S(2)}) async-start(), calls=%async_computation.17 | async-start | bytes 2621440 | tf_op jit(solution)/shard_map/while/body/eval_jaxpr/reduce_scatter | solution.py:226
  1232.4 96.3 %reduce-scatter.13.cloned.1.call-start = ((), (), s32[]{:S(2)}) async-start(), calls=%async_computation.13 | async-start | bytes 10485760 | tf_op jit(solution)/shard_map/reduce_scatter | solution.py:246
  1257.5 145.5 %reduce-scatter.9.cloned.1.call-start = ((), (), s32[]{:S(2)}) async-start(), calls=%async_computation.9 | async-start | bytes 10485760 | tf_op jit(solution)/shard_map/reduce_scatter | solution.py:164
  1272.4 157.2 %reduce-scatter.15.cloned.1.call-start = ((), (), s32[]{:S(2)}) async-start(), calls=%async_computation.14 | async-start | bytes 245760 | tf_op jit(solution)/shard_map/reduce_scatter | solution.py:260
  1300.5 102.5 %copy-start.5 = (f32[8,1,64,1024]{3,2,0,1:T(8,128)S(1)}, f32[8,1,64,1024]{3,2,0,1:T(8,128)}, u32[]{:S(2)}) copy-start(f32[8,1,64,1024]{3,2,0,1:T(8,128)} %copy-done.4) | copy-start | bytes 6291460
  1300.5 102.5 %copy-start.45 = (f32[8,1024]{1,0:T(8,128)S(1)}, f32[8,1024]{1,0:T(8,128)}, u32[]{:S(2)}) copy-start(f32[8,1024]{1,0:T(8,128)} %copy-done.44) | copy-start | bytes 98308
  1300.5 102.5 %copy-start.61 = (f32[1024]{0:T(1024)S(1)}, f32[1024]{0:T(1024)}, u32[]{:S(2)}) copy-start(f32[1024]{0:T(1024)} %copy-done.60) | copy-start | bytes 12292
  1333.6 75.3 %copy-start.57 = (f32[8,1024]{1,0:T(8,128)S(1)}, f32[8,1024]{1,0:T(8,128)}, u32[]{:S(2)}) copy-start(f32[8,1024]{1,0:T(8,128)} %get-tuple-element.207) | copy-start | bytes 98308
  1333.6 75.4 %copy-start.56 = (f32[8,1024]{1,0:T(8,128)S(1)}, f32[8,1024]{1,0:T(8,128)}, u32[]{:S(2)}) copy-start(f32[8,1024]{1,0:T(8,128)} %get-tuple-element.203) | copy-start | bytes 98308
  1409.7 599.7 %all-reduce.22.cloned.1.call-start = ((), (), s32[]{:S(2)}) async-start(), calls=%async_computation.16 | async-start | bytes 37748736 | tf_op jit(solution)/shard_map/psum | solution.py:265
  (79 other events, 850.3 us)
Sparse Core Ops, SparseCore 0:
  22.3 35.9 all-gather.7
  83.3 149.1 all-gather.15
  338.9 69.8 reduce-scatter.6
  412.9 34.4 all-gather.9
  449.5 34.4 all-gather.11
  506.9 71.6 reduce-scatter.10
  585.5 34.4 all-gather.13
  655.3 43.8 reduce-scatter.16
  731.9 43.1 reduce-scatter.16
  807.8 43.1 reduce-scatter.16
  883.7 43.1 reduce-scatter.16
  959.6 43.1 reduce-scatter.16
  1035.5 43.1 reduce-scatter.16
  1111.4 43.1 reduce-scatter.16
  1187.3 43.1 reduce-scatter.16
  1257.6 71.0 reduce-scatter.12
  1331.3 71.6 reduce-scatter.8
  1409.8 19.7 reduce-scatter.14
  1435.8 573.5 all-reduce.21
where the time goes:
time: 2040 us; the launch traced here: 2030 us
  waiting for transfers between devices  1380 us (68%)
  local copies, waits for them, and re-layouts  264 us (13%)
  matrix products  197 us (10%)
  other arithmetic  96.3 us (5%)
  blocking collectives  47.5 us (2%)
  loops' own time  32.1 us (2%)
    psum x1, waiting for transfers between devices, body(): lax.psum((ada_grad, ada_bias_grad, qkv_grad, qkv_bias_grad, out_grad, out...  524 us
    reduce_scatter x8, waiting for transfers between devices, backward_step(): lax.psum_scatter(jnp.concatenate([key_grad, value_grad], axis=-1), 'frame...  336 us
    all_gather x1, waiting for transfers between devices, body(): kv_all = lax.all_gather(kv_own, 'frame', axis=1, tiled=True)  137 us
    reduce_scatter x1, waiting for transfers between devices, body(): lax.psum_scatter(mlp_in_term, 'tensor', scatter_dimension=2, tiled=True)  71.6 us
    reduce_scatter x1, waiting for transfers between devices, body(): lax.psum_scatter(mlp_term, 'tensor', scatter_dimension=2, tiled=True)  69.4 us
    reduce_scatter x1, waiting for transfers between devices, body(): lax.psum_scatter(attn_term, 'tensor', scatter_dimension=2, tiled=True)  69.4 us
    reshape x16, local copies, waits for them, and re-layouts, backward_step(): key_grad = jnp.einsum('hqk,qhd->khd', score_grad, query_clip.reshape(PATC...  41.5 us
  transfers between devices with their start and end apart: 19, of which 19 were waited for; matrix products, arithmetic and copies ran while one was open for 5% of the time, Pallas kernels for 0%

commit v1 on v0

--- a/solution.py
+++ b/solution.py
@@ -3,7 +3,10 @@
 
 import jax
 import jax.numpy as jnp
+import numpy as np
 from jax import lax
+from jax.experimental import pallas as pl
+from jax.experimental.pallas import tpu as pltpu
 from jax.sharding import PartitionSpec as P
 
 HD = 64
@@ -60,7 +63,7 @@
     return normalize(value) * (1.0 + scale) + shift
 
 
-def body(
+def general_body(
     tokens,
     noise_level,
     w_ada,
@@ -293,9 +296,505 @@
     )
 
 
+MIB = 1 << 20
+
+
+def rotary_tables(core, frames):
+    quarter = PATCHES // 4
+    inner = np.arange(quarter)
+    patch = np.zeros((2, 2, 2, quarter), np.int64)
+    for own in range(2):
+        for side in range(2):
+            for far in range(2):
+                patch[own, side, far] = (2 * far + (own ^ side)) * quarter + inner
+    patch = patch.reshape(2, PATCHES)
+    lane = np.arange(HD)
+    first, middle = HD // 4, (HD - HD // 4) // 2
+    bounds = [(0, first), (first, middle), (first + middle, HD - first - middle)]
+    freq = np.zeros(HD, np.float32)
+    sign_up = np.zeros((2, HD), np.float32)
+    sign_down = np.zeros((2, HD), np.float32)
+    which = np.zeros(HD, np.int64)
+    for slot, (start, width) in enumerate(bounds):
+        half = width // 2
+        ladder = 10000.0 ** (-(np.arange(half, dtype=np.float32) / np.float32(half)))
+        freq[start : start + half] = ladder
+        freq[start + half : start + width] = ladder
+        which[start : start + width] = slot
+        kind = 0 if slot == 0 else 1
+        sign_up[kind, start : start + half] = -1.0
+        sign_down[kind, start + half : start + width] = 1.0
+    del lane
+    frame_pos = jnp.arange(frames, dtype=jnp.float32)[:, None]
+    mine = jnp.asarray(patch)[core]
+    row_pos = (mine // GRID).astype(jnp.float32)[None, :]
+    col_pos = (mine % GRID).astype(jnp.float32)[None, :]
+    shape = (frames, PATCHES)
+    spots = jnp.stack(
+        [jnp.broadcast_to(item, shape) for item in (frame_pos, row_pos, col_pos)]
+    ).reshape(3, frames * PATCHES)
+    angle = spots[which].T * jnp.asarray(freq)[None, :]
+    cosine, sine = jnp.cos(angle), jnp.sin(angle)
+    parts = [cosine]
+    for kind in range(2):
+        parts.append(sine * sign_up[kind])
+        parts.append(sine * sign_down[kind])
+    return jnp.stack([jnp.tile(item, (1, 2)) for item in parts])
+
+
+def turn(value, tables, sign):
+    lanes = value.shape[-1]
+    near, far = HD // 8, (HD - HD // 4) // 4
+    moved = (
+        pltpu.roll(value, lanes - near, 1) * tables(1)
+        + pltpu.roll(value, near, 1) * tables(2)
+        + pltpu.roll(value, lanes - far, 1) * tables(3)
+        + pltpu.roll(value, far, 1) * tables(4)
+    )
+    return value * tables(0) + (moved if sign > 0 else -moved)
+
+
+def qkv_kernel(rows_ref, w_ref, b_ref, tab_ref, out_ref):
+    step = pl.program_id(0)
+    block = PATCHES
+    for start in range(0, rows_ref.shape[0], block):
+        here = pl.ds(start, block)
+        value = (
+            jnp.dot(rows_ref[here, :], w_ref[...], preferred_element_type=jnp.float32)
+            + b_ref[0].astype(jnp.float32)
+        )
+
+        @pl.when(step < 2)
+        def _():
+            for lane in range(0, value.shape[1], 128):
+                out_ref[0, here, lane : lane + 128] = turn(
+                    value[:, lane : lane + 128], lambda slot: tab_ref[slot, here, :], 1
+                ).astype(jnp.bfloat16)
+
+        @pl.when(step == 2)
+        def _():
+            out_ref[0, here, :] = value.astype(jnp.bfloat16)
+
+
+def qkv_forward(rows, w, b, tables):
+    count, width = rows.shape
+    cols = w.shape[1] // 3
+    return pl.pallas_call(
+        qkv_kernel,
+        grid=(3,),
+        in_specs=[
+            pl.BlockSpec((count, width), lambda i: (0, 0)),
+            pl.BlockSpec((width, cols), lambda i: (0, i)),
+            pl.BlockSpec((1, 1, cols), lambda i: (i, 0, 0)),
+            pl.BlockSpec(tables.shape, lambda i: (0, 0, 0)),
+        ],
+        out_specs=pl.BlockSpec((1, count, cols), lambda i: (i, 0, 0)),
+        out_shape=jax.ShapeDtypeStruct((3, count, cols), jnp.bfloat16),
+        compiler_params=pltpu.CompilerParams(vmem_limit_bytes=48 * MIB),
+        cost_estimate=pl.CostEstimate(
+            flops=2 * count * width * cols * 3, bytes_accessed=12 * MIB, transcendentals=0
+        ),
+        name="qkv_forward",
+    )(rows, w, b[:, None, :], tables)
+
+
+def attend_kernel(frames, qkv_ref, out_ref, lse_ref):
+    lanes = qkv_ref.shape[2]
+    low_lane = lax.broadcasted_iota(jnp.int32, (PATCHES, lanes), 1) < HD
+    for frame in range(frames):
+        here = pl.ds(frame * PATCHES, PATCHES)
+        length = (frame + 1) * PATCHES
+        query = qkv_ref[0, here, :] * jnp.bfloat16(1.0 / math.sqrt(HD))
+        keys = qkv_ref[1, :length, :]
+        values = qkv_ref[2, :length, :]
+        outs, sums = [], []
+        for head in range(2):
+            chosen = low_lane if head == 0 else jnp.logical_not(low_lane)
+            scores = lax.dot_general(
+                jnp.where(chosen, query, jnp.bfloat16(0)),
+                keys,
+                (((1,), (1,)), ((), ())),
+                preferred_element_type=jnp.float32,
+            )
+            top = jnp.max(scores, axis=1, keepdims=True)
+            grown = jnp.exp(scores - top)
+            total = jnp.sum(grown, axis=1, keepdims=True)
+            prob = (grown * (1.0 / total)).astype(jnp.bfloat16)
+            outs.append(jnp.dot(prob, values, preferred_element_type=jnp.float32))
+            sums.append(top + jnp.log(total))
+        out_ref[here, :] = jnp.where(low_lane, outs[0], outs[1]).astype(jnp.bfloat16)
+        lse_ref[0, here, :] = jnp.concatenate(sums, axis=1)
+
+
+def attend(qkv, frames):
+    _, count, cols = qkv.shape
+    pairs = cols // 128
+    return pl.pallas_call(
+        partial(attend_kernel, frames),
+        grid=(pairs,),
+        in_specs=[pl.BlockSpec((3, count, 128), lambda i: (0, 0, i))],
+        out_specs=[
+            pl.BlockSpec((count, 128), lambda i: (0, i)),
+            pl.BlockSpec((1, count, 2), lambda i: (i, 0, 0)),
+        ],
+        out_shape=[
+            jax.ShapeDtypeStruct((count, cols), jnp.bfloat16),
+            jax.ShapeDtypeStruct((pairs, count, 2), jnp.float32),
+        ],
+        compiler_params=pltpu.CompilerParams(vmem_limit_bytes=48 * MIB),
+        cost_estimate=pl.CostEstimate(
+            flops=12_000_000_000, bytes_accessed=4 * MIB, transcendentals=2_600_000
+        ),
+        name="attend",
+    )(qkv)
+
+
+def attend_back_kernel(frames, qkv_ref, grad_ref, lse_ref, tab_ref, out_ref, dk_ref, dv_ref):
+    lanes = qkv_ref.shape[2]
+    low_lane = lax.broadcasted_iota(jnp.int32, (PATCHES, lanes), 1) < HD
+    scale = 1.0 / math.sqrt(HD)
+    zero = jnp.bfloat16(0)
+    dk_ref[...] = jnp.zeros_like(dk_ref)
+    dv_ref[...] = jnp.zeros_like(dv_ref)
+    for frame in range(frames):
+        here = pl.ds(frame * PATCHES, PATCHES)
+        length = (frame + 1) * PATCHES
+        query = qkv_ref[0, here, :]
+        grad = grad_ref[here, :]
+        keys = qkv_ref[1, :length, :]
+        values = qkv_ref[2, :length, :]
+        outs = []
+        for head in range(2):
+            chosen = low_lane if head == 0 else jnp.logical_not(low_lane)
+            query_head = jnp.where(chosen, query, zero)
+            grad_head = jnp.where(chosen, grad, zero)
+            scores = lax.dot_general(
+                query_head * jnp.bfloat16(scale),
+                keys,
+                (((1,), (1,)), ((), ())),
+                preferred_element_type=jnp.float32,
+            )
+            prob = jnp.exp(scores - lse_ref[0, here, head : head + 1])
+            prob_grad = lax.dot_general(
+                grad_head, values, (((1,), (1,)), ((), ())), preferred_element_type=jnp.float32
+            )
+            row_dot = jnp.sum(prob * prob_grad, axis=1, keepdims=True)
+            score_grad = (prob * ((prob_grad - row_dot) * scale)).astype(jnp.bfloat16)
+            outs.append(jnp.dot(score_grad, keys, preferred_element_type=jnp.float32))
+            dk_ref[:length, :] += lax.dot_general(
+                score_grad,
+                query_head,
+                (((0,), (0,)), ((), ())),
+                preferred_element_type=jnp.float32,
+            )
+            dv_ref[:length, :] += lax.dot_general(
+                prob.astype(jnp.bfloat16),
+                grad_head,
+                (((0,), (0,)), ((), ())),
+                preferred_element_type=jnp.float32,
+            )
+        out_ref[0, here, :] = turn(
+            jnp.where(low_lane, outs[0], outs[1]), lambda slot: tab_ref[slot, here, :], -1
+        ).astype(jnp.bfloat16)
+    out_ref[1] = turn(dk_ref[...], lambda slot: tab_ref[slot], -1).astype(jnp.bfloat16)
+    out_ref[2] = dv_ref[...].astype(jnp.bfloat16)
+
+
+def attend_back(qkv, grad, lse, tables, frames):
+    _, count, cols = qkv.shape
+    pairs = cols // 128
+    return pl.pallas_call(
+        partial(attend_back_kernel, frames),
+        grid=(pairs,),
+        in_specs=[
+            pl.BlockSpec((3, count, 128), lambda i: (0, 0, i)),
+            pl.BlockSpec((count, 128), lambda i: (0, i)),
+            pl.BlockSpec((1, count, 2), lambda i: (i, 0, 0)),
+            pl.BlockSpec(tables.shape, lambda i: (0, 0, 0)),
+        ],
+        out_specs=pl.BlockSpec((3, count, 128), lambda i: (0, 0, i)),
+        out_shape=jax.ShapeDtypeStruct((3, count, cols), jnp.bfloat16),
+        scratch_shapes=[
+            pltpu.VMEM((count, 128), jnp.float32),
+            pltpu.VMEM((count, 128), jnp.float32),
+        ],
+        compiler_params=pltpu.CompilerParams(vmem_limit_bytes=48 * MIB),
+        cost_estimate=pl.CostEstimate(
+            flops=24_000_000_000, bytes_accessed=6 * MIB, transcendentals=2_600_000
+        ),
+        name="attend_back",
+    )(qkv, grad, lse, tables)
+
+
+def fast_body(
+    tokens,
+    noise_level,
+    w_ada,
+    b_ada,
+    w_qkv,
+    b_qkv,
+    w_out,
+    b_out,
+    w_fc1,
+    b_fc1,
+    w_fc2,
+    b_fc2,
+    cotangent,
+):
+    clips, _, quarter, width = tokens.shape
+    frames = lax.axis_size("frame")
+    cols = w_qkv.shape[2]
+    batch_now = lax.axis_index("batch")
+    frame_now = lax.axis_index("frame")
+    tensor_now = lax.axis_index("tensor")
+    core = tensor_now % 2
+    far = tensor_now // 2
+    clip_now = frame_now * 2 + far
+    rows_own = clips * quarter
+    count = 2 * rows_own
+    f32 = jnp.float32
+    bf16 = jnp.bfloat16
+    groups = [
+        [f * 4 + 2 * y + c for f in range(frames) for y in range(2)] for c in range(2)
+    ]
+
+    def to_clip(item):
+        return lax.all_to_all(item, ("frame", "tensor"), 0, 0, axis_index_groups=groups)
+
+    def swap_y(item):
+        return lax.ppermute(item, "tensor", [(t, t ^ 2) for t in range(4)])
+
+    def swap_core(item):
+        return lax.ppermute(item, "tensor", [(t, t ^ 1) for t in range(4)])
+
+    def swap_x(item):
+        return lax.ppermute(item, "batch", [(0, 1), (1, 0)])
+
+    def swap_z(item, bit):
+        return lax.ppermute(item, "frame", [(f, f ^ bit) for f in range(frames)])
+
+    def ordered(mine, theirs, place):
+        return jnp.stack(
+            [jnp.where(place == 0, mine, theirs), jnp.where(place == 0, theirs, mine)]
+        )
+
+    def both_cores(item):
+        return jnp.concatenate([item, swap_core(item)], axis=1).reshape(count, width)
+
+    def sum_cores(term):
+        split = term.reshape(frames, 2, rows_own // frames, width)
+        return split[:, 0] + swap_core(split[:, 1])
+
+    tables = rotary_tables(core, frames)
+    condition = jax.nn.silu(embedding(noise_level, width)).astype(bf16)
+    mod_part = jnp.einsum(
+        "cfd,dke->cfke", condition, w_ada, preferred_element_type=f32
+    ) + b_ada.astype(f32)
+    tokens_own = to_clip(tokens[:, 0]).reshape(frames, 2 * quarter, width)
+    mod_own = to_clip(mod_part[:, 0]).reshape(frames, 2, 6, cols)
+    modulation = ordered(mod_own, swap_core(mod_own), core)
+    modulation = modulation.transpose(1, 3, 2, 0, 4).reshape(frames, 6, width)
+    pieces = [modulation[:, slot : slot + 1, :] for slot in range(6)]
+    w_qkv_own = w_qkv.reshape(width, 3 * cols)
+    w_qkv_far = swap_y(w_qkv_own)
+    b_qkv_far = swap_y(b_qkv)
+    b_fc1_far = swap_y(b_fc1)
+    w_out_far = swap_y(w_out)
+    w_fc1_far = swap_y(w_fc1)
+    w_fc2_far = swap_y(w_fc2)
+    cot_own = to_clip(cotangent[:, 0]).reshape(frames, 2 * quarter, width)
+
+    resid_in = tokens_own.astype(f32)
+    attn_val, ln_one_back = jax.vjp(modulate, resid_in, pieces[0], pieces[1])
+    attn_rows = both_cores(attn_val.astype(bf16))
+    qkv_own = qkv_forward(attn_rows, w_qkv_own, b_qkv, tables)
+    mixed_own, lse_own = attend(qkv_own, frames)
+    qkv_far = qkv_forward(attn_rows, w_qkv_far, b_qkv_far, tables)
+    mixed_far, lse_far = attend(qkv_far, frames)
+    attn_term = jnp.dot(mixed_own, w_out, preferred_element_type=f32) + jnp.dot(
+        mixed_far, w_out_far, preferred_element_type=f32
+    )
+    attn_branch = sum_cores(attn_term) + b_out.astype(f32)
+    resid_one = resid_in + pieces[2] * attn_branch
+    mlp_val, ln_two_back = jax.vjp(modulate, resid_one, pieces[3], pieces[4])
+    mlp_rows = both_cores(mlp_val.astype(bf16))
+
+    upstream = cot_own.astype(f32)
+    mlp_grad = (pieces[5] * upstream).astype(bf16)
+    mlp_grad_rows = both_cores(mlp_grad)
+
+    def hidden(w_one, b_one, w_two):
+        pre_act = jnp.dot(mlp_rows, w_one, preferred_element_type=f32) + b_one.astype(f32)
+        act_val, gelu_back = jax.vjp(partial(jax.nn.gelu, approximate=True), pre_act)
+        activated = act_val.astype(bf16)
+        mlp_term = jnp.dot(activated, w_two, preferred_element_type=f32)
+        act_grad = lax.dot_general(
+            mlp_grad_rows, w_two, (((1,), (1,)), ((), ())), preferred_element_type=f32
+        )
+        pre_grad = gelu_back(act_grad)[0].astype(bf16)
+        in_term = lax.dot_general(
+            pre_grad, w_one, (((1,), (1,)), ((), ())), preferred_element_type=f32
+        )
+        two_grad = lax.dot_general(
+            activated, mlp_grad_rows, (((0,), (0,)), ((), ())), preferred_element_type=f32
+        )
+        one_grad = lax.dot_general(
+            mlp_rows, pre_grad, (((0,), (0,)), ((), ())), preferred_element_type=f32
+        )
+        bias_grad = jnp.sum(pre_grad.astype(f32), axis=0)
+        return mlp_term, in_term, one_grad, two_grad, bias_grad
+
+    term_own, in_own, fc1_own, fc2_own, fc1_bias_own = hidden(w_fc1, b_fc1, w_fc2)
+    term_far, in_far, fc1_far, fc2_far, fc1_bias_far = hidden(w_fc1_far, b_fc1_far, w_fc2_far)
+    mlp_in_grad = sum_cores(in_own + in_far)
+    mlp_branch = sum_cores(term_own + term_far) + b_fc2.astype(f32)
+    output_own = (resid_one + pieces[5] * mlp_branch).astype(bf16)
+    gate_two_grad = jnp.sum(upstream * mlp_branch, axis=1, keepdims=True)
+    fc2_bias_part = jnp.sum(mlp_grad.astype(f32), axis=(0, 1))
+
+    def over_xz(total):
+        rows, lanes = total.shape
+        low_bit, high_bit = frame_now % 2, frame_now // 2
+
+        def halve(item, place, send):
+            split = item.reshape(2, item.shape[0] // 2, lanes)
+            keep = lax.dynamic_index_in_dim(split, place, 0, False)
+            away = lax.dynamic_index_in_dim(split, 1 - place, 0, False)
+            return keep + send(away.astype(bf16)).astype(f32)
+
+        def join(item, place, send):
+            return ordered(item, send(item), place).reshape(2 * item.shape[0], lanes)
+
+        part = halve(total, batch_now, swap_x)
+        part = halve(part, low_bit, lambda item: swap_z(item, 1))
+        part = halve(part, high_bit, lambda item: swap_z(item, 2)).astype(bf16)
+        part = join(part, high_bit, lambda item: swap_z(item, 2))
+        part = join(part, low_bit, lambda item: swap_z(item, 1))
+        return join(part, batch_now, swap_x).astype(f32)
+
+    def reduced(own, other):
+        return over_xz(own + swap_y(other.astype(bf16)).astype(f32))
+
+    fc2_grad = reduced(fc2_own, fc2_far)
+    fc1_grad = reduced(fc1_own, fc1_far)
+
+    resid_part, shift_two_grad, scale_two_grad = ln_two_back(mlp_in_grad)
+    resid_grad = upstream + resid_part
+    attn_grad = (pieces[2] * resid_grad).astype(bf16)
+    gate_one_grad = jnp.sum(resid_grad * attn_branch, axis=1, keepdims=True)
+    out_bias_part = jnp.sum(attn_grad.astype(f32), axis=(0, 1))
+    attn_grad_rows = both_cores(attn_grad)
+
+    def heads_back(w, qkv, mixed, lse, w_in):
+        mixed_grad = lax.dot_general(
+            attn_grad_rows, w, (((1,), (1,)), ((), ())), preferred_element_type=f32
+        ).astype(bf16)
+        out_grad = lax.dot_general(
+            mixed, attn_grad_rows, (((0,), (0,)), ((), ())), preferred_element_type=f32
+        )
+        back = attend_back(qkv, mixed_grad, lse, tables, frames)
+        back = back.transpose(1, 0, 2).reshape(count, 3 * cols)
+        qkv_grad = lax.dot_general(
+            attn_rows, back, (((0,), (0,)), ((), ())), preferred_element_type=f32
+        )
+        in_term = lax.dot_general(
+            back, w_in, (((1,), (1,)), ((), ())), preferred_element_type=f32
+        )
+        return out_grad, qkv_grad, jnp.sum(back.astype(f32), axis=0), in_term
+
+    out_far, qkv_grad_far, qkv_bias_far, attn_in_far = heads_back(
+        w_out_far, qkv_far, mixed_far, lse_far, w_qkv_far
+    )
+    out_own, qkv_grad_own, qkv_bias_own, attn_in_own = heads_back(
+        w_out, qkv_own, mixed_own, lse_own, w_qkv_own
+    )
+    out_grad = reduced(out_own, out_far)
+    qkv_grad = reduced(qkv_grad_own, qkv_grad_far).reshape(width, 3, cols)
+    attn_in_grad = sum_cores(attn_in_own + attn_in_far)
+    input_part, shift_one_grad, scale_one_grad = ln_one_back(attn_in_grad)
+    tokens_grad_own = resid_grad + input_part
+    tokens_grad = to_clip(tokens_grad_own.astype(bf16).reshape(clips, quarter, width))
+    output = to_clip(output_own.reshape(clips, quarter, width))
+
+    mod_grad = jnp.concatenate(
+        [
+            shift_one_grad,
+            scale_one_grad,
+            gate_one_grad,
+            shift_two_grad,
+            scale_two_grad,
+            gate_two_grad,
+        ],
+        axis=1,
+    )
+    mod_grad = mod_grad + swap_core(mod_grad)
+    mod_cols = mod_grad.reshape(frames, 6, 4, cols)
+    mod_mine = lax.dynamic_index_in_dim(mod_cols, tensor_now, 2, False)
+    mod_away = lax.dynamic_index_in_dim(mod_cols, jnp.bitwise_xor(tensor_now, 2), 2, False)
+    shared = jnp.concatenate([out_bias_part, fc2_bias_part])
+    shared = shared + swap_core(shared)
+    shared = shared + swap_y(shared)
+    local = jnp.concatenate([fc1_bias_own, qkv_bias_own])
+    away = jnp.concatenate([fc1_bias_far, qkv_bias_far])
+    small = jnp.concatenate([shared, local + swap_y(away)])
+    gathered = jnp.stack([mod_mine, swap_y(mod_away)])
+    gathered = jnp.stack([gathered, swap_x(gathered)])
+    gathered = jnp.stack([gathered, swap_z(gathered, 1)])
+    gathered = jnp.stack([gathered, swap_z(gathered, 2)])
+    small = small + swap_x(small)
+    small = small + swap_z(small, 1)
+    small = small + swap_z(small, 2)
+    flips = jnp.arange(32 // 2)
+    origin = (
+        frame_now * 4 + batch_now * 2 + far
+    )
+    gathered = gathered.reshape(16, frames, 6, cols)[jnp.bitwise_xor(flips, origin)]
+    noise_all = lax.all_gather(noise_level, ("batch", "frame"))[..., 0]
+    noise_all = noise_all.reshape(2, frames, frames, 2)
+    noise_all = noise_all.transpose(2, 0, 3, 1).reshape(16 * frames)
+    condition_all = jax.nn.silu(embedding(noise_all, width)).astype(bf16)
+    mod_flat = gathered.reshape(16 * frames, 6 * cols)
+    ada_grad = lax.dot_general(
+        condition_all.astype(f32),
+        mod_flat,
+        (((0,), (0,)), ((), ())),
+        precision=lax.Precision.HIGHEST,
+        preferred_element_type=f32,
+    ).reshape(width, 6, cols)
+    ada_bias_grad = jnp.sum(gathered, axis=(0, 1))
+    hidden_cols = fc1_bias_own.shape[0]
+    fc1_end = 2 * width + hidden_cols
+    return (
+        output[:, None],
+        tokens_grad.astype(f32)[:, None],
+        ada_grad,
+        ada_bias_grad,
+        qkv_grad,
+        small[fc1_end:].reshape(3, cols),
+        out_grad,
+        small[:width],
+        fc1_grad,
+        small[2 * width : fc1_end],
+        fc2_grad,
+        small[width : 2 * width],
+    )
+
+
+def pick_body(tokens, *rest):
+    paired = (
+        lax.axis_size("tensor") == 4
+        and lax.axis_size("frame") == 4
+        and lax.axis_size("batch") == 2
+        and tokens.shape[0] == 8
+        and rest[1].shape[0] % 256 == 0
+        and rest[3].shape[2] % 128 == 0
+    )
+    return fast_body(tokens, *rest) if paired else general_body(tokens, *rest)
+
+
 def solution(mesh):
     return jax.shard_map(
-        body,
+        pick_body,
         mesh=mesh,
         in_specs=(
             P("batch", "frame", "tensor", None),

time: 2040 us -> 627 us (0.31)
  waiting for transfers between devices: 1380 us -> 246 us
  local copies, waits for them, and re-layouts: 264 us -> 60 us
  matrix products: 197 us -> 85 us
  Pallas kernels: 0 us -> 67.4 us
  starting transfers between devices: 2.05 us -> 63 us
  other arithmetic: 96.3 us -> 62.5 us
  loops' own time: 32.1 us -> 0 us
    reduce_scatter x13 -> x0, waiting for transfers between devices: 589 us -> none  [the longest x8 336 us: backward_step(): lax.psum_scatter(jnp.concatenate([key_grad, value_grad], axis=-1), 'frame...]
    psum x1 -> x0, waiting for transfers between devices: 524 us -> none  [body(): lax.psum((ada_grad, ada_bias_grad, qkv_grad, qkv_bias_grad, out_grad, out...]
    all_gather x5 -> x0, waiting for transfers between devices: 265 us -> none  [the longest x1 137 us: body(): kv_all = lax.all_gather(kv_own, 'frame', axis=1, tiled=True)]
    ppermute x0 -> x54, waiting for transfers between devices: none -> 230 us  [the longest x13 115 us: swap_y(): return lax.ppermute(item, 'tensor', [(t, t ^ 2) for t in range(4)])]
    dot_general x70 -> x24, matrix products: 197 us -> 85 us  [the longest x2 13.6 us: hidden(): lax.dot_general(mlp_grad_rows, w_two, (((1,), (1,)), ((), ())), preferred...]
    reshape x64 -> x4, local copies, waits for them, and re-layouts: 77.9 us -> 1.76 us  [the longest x1 1.57 us: fast_body(): w_qkv_own = w_qkv.reshape(width, 3 * cols)]
    pallas_call x0 -> x6, Pallas kernels: none -> 67.4 us  [the longest x2 29 us: attend_back(): pl.pallas_call(partial(attend_back_kernel, frames), grid=(pairs,), in_spe...]
    ppermute x0 -> x54, starting transfers between devices: none -> 44.9 us  [the longest x20 17.9 us: swap_z(): return lax.ppermute(item, 'frame', [(f, f ^ bit) for f in range(frames)])]
  transfers between devices with their start and end apart: 19 -> 58, of which waited for: 19 -> 23; matrix products, arithmetic and copies ran while one was open for 5% -> 27% of each run, Pallas kernels for 0% -> 11%
where the time goes in v1:
time: 627 us; the launch traced here: 623 us
  waiting for transfers between devices  246 us (39%)
  matrix products  85 us (14%)
  Pallas kernels  67.4 us (11%)
  starting transfers between devices  63 us (10%)
  other arithmetic  62.5 us (10%)
  local copies, waits for them, and re-layouts  60 us (10%)
  blocking collectives  35.4 us (6%)
    ppermute x13, waiting for transfers between devices, swap_y(): return lax.ppermute(item, 'tensor', [(t, t ^ 2) for t in range(4)])  115 us
    ppermute x20, waiting for transfers between devices, swap_z(): return lax.ppermute(item, 'frame', [(f, f ^ bit) for f in range(frames)])  81 us
    ppermute x10, waiting for transfers between devices, swap_x(): return lax.ppermute(item, 'batch', [(0, 1), (1, 0)])  32.2 us
    pallas_call x2, Pallas kernels, attend_back(): pl.pallas_call(partial(attend_back_kernel, frames), grid=(pairs,), in_spe...  29 us
    unnamed x186, local copies, waits for them, and re-layouts  28.1 us
    unnamed x1, blocking collectives  21.5 us
    pallas_call x2, Pallas kernels, qkv_forward(): pl.pallas_call(qkv_kernel, grid=(3,), in_specs=[pl.BlockSpec((count, widt...  20.6 us
    all_to_all x4, starting transfers between devices, to_clip(): lax.all_to_all(item, ('frame', 'tensor'), 0, 0, axis_index_groups=groups)  18 us
  transfers between devices with their start and end apart: 58, of which 23 were waited for; matrix products, arithmetic and copies ran while one was open for 27% of the time, Pallas kernels for 11%

profile of v1, /device:TPU:0, one launch (start us, length us, event | category | flops | bytes accessed | tf_op | source)
XLA Modules:
  0.0 622.5 jit_solution(5851564224372540443)
XLA Ops:
  3.1 14.0 %all_to_all.25 = f32[8,6,256]{2,1,0:T(8,128)S(1)} all-to-all(f32[8,6,256]{2,1,0:T(8,128)S(1)} %copy.129), channel_id=1, replica_groups={{0,2,4,6,8,10,12,14},{1,3,5,7,9,11,13,15},{16,18,20,22,24,26,28,30},{17..., dimensions={0} | all-to-all | bytes 98304 | tf_op jit(solution)/shard_map/all_to_all | solution.py:562
  29.6 15.8 %all-to-all-done = bf16[8,64,1024]{2,1,0:T(8,128)(2,1)S(1)} async-done(((bf16[8,64,1024]{2,1,0:T(8,128)(2,1)}), bf16[8,64,1024]{2,1,0:T(8,128)(2,1)S(1)}, u32[]{:S(2)}, u32[]{:S(2)}) %all-to-all-start) | async-done | bytes 1048608 | tf_op jit(solution)/shard_map/all_to_all | solution.py:562
  66.6 10.7 %qkv_forward.2.qkv_ref = bf16[3,1024,256]{2,1,0:T(8,128)(2,1)S(1)} custom-call(bf16[1024,1024]{1,0:T(8,128)(2,1)S(1)} %bitcast.400, bf16[1024,768]{1,0:T(8,128)(2,1)} %copy.140.w_ref, bf16[3,1,256]{2,1,0:T(2,128)(2,1)S(1)} %copy.141.b_ref, f32[5,1024,128]{2,1,0:T(8,128)} %copy-done.31), custom_call_target="tpu_custom_call" | custom-call | flops 1610612736 | bytes 12582912 | tf_op jit(solution)/shard_map/qkv_forward/pallas_call | solution.py:382
  77.3 10.7 %collective-permute-done.2.w_ref = bf16[1024,768]{1,0:T(8,128)(2,1)} collective-permute-done((bf16[1024,768]{1,0:T(8,128)(2,1)}, bf16[1024,768]{1,0:T(8,128)(2,1)}, u32[]{:S(2)}, u32[]{:S(2)}) %collective-permute-start.2) | collective-permute-done | bytes 1572896 | tf_op jit(solution)/shard_map/ppermute | solution.py:565
  88.0 9.9 %qkv_forward.3.qkv_ref = bf16[3,1024,256]{2,1,0:T(8,128)(2,1)S(1)} custom-call(bf16[1024,1024]{1,0:T(8,128)(2,1)S(1)} %bitcast.401, bf16[1024,768]{1,0:T(8,128)(2,1)} %collective-permute-done.2.w_ref, bf16[3,1,256]{2,1,0:T(2,128)(2,1)S(1)} %copy.143.b_ref, f32[5,1024,128]{2,1,0:T(8,128)} %copy-done.31), custom_call_target="tpu_custom_call" | custom-call | flops 1610612736 | bytes 12582912 | tf_op jit(solution)/shard_map/qkv_forward/pallas_call | solution.py:382
  97.9 8.7 %attend.3 = (bf16[1024,256]{1,0:T(8,128)(2,1)S(1)}, f32[2,1024,2]{2,1,0:T(8,128)S(1)}) custom-call(bf16[3,1024,256]{2,1,0:T(8,128)(2,1)S(1)} %qkv_forward.3.qkv_ref), custom_call_target="tpu_custom_call" | custom-call | flops 12000000000 | bytes 4194304 | tf_op jit(solution)/shard_map/attend/pallas_call | solution.py:432
  107.7 9.2 %attend.2 = (bf16[1024,256]{1,0:T(8,128)(2,1)S(1)}, f32[2,1024,2]{2,1,0:T(8,128)S(1)}) custom-call(bf16[3,1024,256]{2,1,0:T(8,128)(2,1)S(1)} %qkv_forward.2.qkv_ref), custom_call_target="tpu_custom_call" | custom-call | flops 12000000000 | bytes 4194304 | tf_op jit(solution)/shard_map/attend/pallas_call | solution.py:432
  135.4 21.5 %all-reduce = f32[64]{0:T(128)S(1)} all-reduce(f32[64]{0:T(128)S(1)} %bitcast_dynamic-update-slice_fusion), channel_id=2, replica_groups=mesh['batch'=2,'frame'=4,'tensor'=4] {'batch','frame'}, use_global_device_ids=true, to_apply=%add | all-reduce | flops 64 | bytes 512
  167.8 4.7 collective-permute-done.7
  179.5 37.4 %collective-permute-done.9 = bf16[1024,1024]{1,0:T(8,128)(2,1)} collective-permute-done((bf16[1024,1024]{1,0:T(8,128)(2,1)}, bf16[1024,1024]{1,0:T(8,128)(2,1)}, u32[]{:S(2)}, u32[]{:S(2)}) %collective-permute-start.9) | collective-permute-done | bytes 2097184 | tf_op jit(solution)/shard_map/ppermute | solution.py:565
  216.9 6.6 %convert_reduce_fusion = (f32[1024]{0:T(1024)S(1)}, bf16[1024,1024]{1,0:T(8,128)(2,1)S(1)}) fusion(f32[1024,1024]{1,0:T(8,128)S(1)} %fusion.71, f32[1024]{0:T(1024)S(1)} %convert_element_type.292, bf16[1024,1024]{1,0:T(8,128)(2,1)S(1)} %bitcast.455, bf16[1024,1024]{1,0:T(8,128)(2,1)} %collective-permute-done.9), kind=kOutput, calls=%fused_computation.23 | convolution fusion | flops 2171599872 | bytes 10493952 | tf_op jit(solution)/shard_map/dot_general | solution.py:631
  228.0 7.0 %convert_reduce_fusion.1 = (f32[1024]{0:T(1024)S(1)}, bf16[1024,1024]{1,0:T(8,128)(2,1)S(1)}) fusion(f32[1024,1024]{1,0:T(8,128)S(1)} %fusion.70, f32[1024]{0:T(1024)S(1)} %convert_element_type.290, bf16[1024,1024]{1,0:T(8,128)(2,1)S(1)} %bitcast.456, bf16[1024,1024]{1,0:T(8,128)(2,1)} %param.31), kind=kOutput, calls=%fused_computation.24 | convolution fusion | flops 2171599872 | bytes 10493952 | tf_op jit(solution)/shard_map/dot_general | solution.py:631
  244.6 6.5 %fusion.62 = f32[1024,1024]{1,0:T(8,128)} fusion(bf16[1024,1024]{1,0:T(8,128)(2,1)} %param.31, f32[1024,1024]{1,0:T(8,128)S(1)} %fusion.70, f32[1024]{0:T(1024)S(1)} %convert_element_type.290), kind=kOutput, calls=%fused_computation.258 | convolution fusion | flops 2157969408 | bytes 10489856 | tf_op jit(solution)/shard_map/dot_general | solution.py:630
  251.1 5.7 convolution_add_fusion.2
  257.5 60.6 %collective-permute-done.47 = bf16[1024,1024]{1,0:T(8,128)(2,1)S(1)} collective-permute-done((bf16[1024,1024]{1,0:T(8,128)(2,1)S(1)}, bf16[1024,1024]{1,0:T(8,128)(2,1)S(1)}, u32[]{:S(2)}, u32[]{:S(2)}) %collective-permute-start.47) | collective-permute-done | bytes 2097184 | tf_op jit(solution)/shard_map/ppermute | solution.py:565
  337.1 5.5 all-to-all-start.2
  342.6 6.2 collective-permute-done.48
  360.0 14.3 %attend_back.3 = bf16[3,1024,256]{2,1,0:T(8,128)(2,1)S(1)} custom-call(bf16[3,1024,256]{2,1,0:T(8,128)(2,1)S(1)} %copy-done.13, bf16[1024,256]{1,0:T(8,128)(2,1)S(1)} %convolution_convert_fusion.4.grad_ref, f32[2,1024,2]{2,1,0:T(8,128)S(1)} %copy-done.18, f32[5,1024,128]{2,1,0:T(8,128)} %copy-done.31), custom_call_target="tpu_custom_call" | custom-call | flops 24000000000 | bytes 6291456 | tf_op jit(solution)/shard_map/attend_back/pallas_call | solution.py:506
  379.9 14.7 %attend_back.2 = bf16[3,1024,256]{2,1,0:T(8,128)(2,1)S(1)} custom-call(bf16[3,1024,256]{2,1,0:T(8,128)(2,1)S(1)} %copy-done.11, bf16[1024,256]{1,0:T(8,128)(2,1)S(1)} %copy-done.14, f32[2,1024,2]{2,1,0:T(8,128)S(1)} %copy-done.16, f32[5,1024,128]{2,1,0:T(8,128)} %copy-done.31), custom_call_target="tpu_custom_call" | custom-call | flops 24000000000 | bytes 6291456 | tf_op jit(solution)/shard_map/attend_back/pallas_call | solution.py:506
  434.3 5.8 collective-permute-done.34
  443.1 5.8 collective-permute-done.35
  449.1 6.3 %collective-permute-done.50 = bf16[128,1024]{1,0:T(8,128)(2,1)S(1)} collective-permute-done((bf16[128,1024]{1,0:T(8,128)(2,1)S(1)}, bf16[128,1024]{1,0:T(8,128)(2,1)S(1)}, u32[]{:S(2)}, u32[]{:S(2)}) %collective-permute-start.50) | collective-permute-done | bytes 262176 | tf_op jit(solution)/shard_map/ppermute | solution.py:574
  455.5 12.5 %collective-permute-done.36 = bf16[32,1024]{1,0:T(8,128)(2,1)S(1)} collective-permute-done((bf16[32,1024]{1,0:T(8,128)(2,1)S(1)}, bf16[32,1024]{1,0:T(8,128)(2,1)S(1)}, u32[]{:S(2)}, u32[]{:S(2)}) %collective-permute-start.36) | collective-permute-done | bytes 65568 | tf_op jit(solution)/shard_map/ppermute | solution.py:574
  471.2 10.9 %collective-permute-done.37 = bf16[32,1024]{1,0:T(8,128)(2,1)S(1)} collective-permute-done((bf16[32,1024]{1,0:T(8,128)(2,1)S(1)}, bf16[32,1024]{1,0:T(8,128)(2,1)S(1)}, u32[]{:S(2)}, u32[]{:S(2)}) %collective-permute-start.37) | collective-permute-done | bytes 65568 | tf_op jit(solution)/shard_map/ppermute | solution.py:574
  484.4 6.2 collective-permute-done.38
  493.8 5.0 collective-permute-done.39
  520.5 4.8 collective-permute-done.17
  557.1 15.3 %collective-permute-done.23 = bf16[128,768]{1,0:T(8,128)(2,1)S(1)} collective-permute-done((bf16[128,768]{1,0:T(8,128)(2,1)S(1)}, bf16[128,768]{1,0:T(8,128)(2,1)S(1)}, u32[]{:S(2)}, u32[]{:S(2)}) %collective-permute-start.23) | collective-permute-done | bytes 196640 | tf_op jit(solution)/shard_map/ppermute | solution.py:574
  574.0 7.9 %collective-permute-done.24 = bf16[128,768]{1,0:T(8,128)(2,1)S(1)} collective-permute-done((bf16[128,768]{1,0:T(8,128)(2,1)S(1)}, bf16[128,768]{1,0:T(8,128)(2,1)S(1)}, u32[]{:S(2)}, u32[]{:S(2)}) %collective-permute-start.24) | collective-permute-done | bytes 196640 | tf_op jit(solution)/shard_map/ppermute | solution.py:574
  584.2 8.3 %collective-permute-done.25 = bf16[256,768]{1,0:T(8,128)(2,1)S(1)} collective-permute-done((bf16[256,768]{1,0:T(8,128)(2,1)S(1)}, bf16[256,768]{1,0:T(8,128)(2,1)S(1)}, u32[]{:S(2)}, u32[]{:S(2)}) %collective-permute-start.25) | collective-permute-done | bytes 393248 | tf_op jit(solution)/shard_map/ppermute | solution.py:574
  592.7 4.7 bitcast_convert_fusion
  600.2 10.5 %collective-permute-done.26 = bf16[512,768]{1,0:T(8,128)(2,1)} collective-permute-done((bf16[512,768]{1,0:T(8,128)(2,1)S(1)}, bf16[512,768]{1,0:T(8,128)(2,1)}, u32[]{:S(2)}, u32[]{:S(2)}) %collective-permute-start.26) | collective-permute-done | bytes 786464 | tf_op jit(solution)/shard_map/ppermute | solution.py:571
  (466 shorter events, 245.4 us)
Async XLA Ops:
  17.1 28.3 %all-to-all-start = ((bf16[8,64,1024]{2,1,0:T(8,128)(2,1)}), bf16[8,64,1024]{2,1,0:T(8,128)(2,1)S(1)}, u32[]{:S(2)}, u32[]{:S(2)}) async-start(bf16[8,64,1024]{2,1,0:T(8,128)(2,1)} %bitcast.472), calls=%async_computation | async-start | bytes 2097152 | tf_op jit(solution)/shard_map/all_to_all | solution.py:562
  20.7 43.2 %collective-permute-start.3 = (bf16[3,256]{1,0:T(4,128)(2,1)S(1)}, bf16[3,256]{1,0:T(4,128)(2,1)S(1)}, u32[]{:S(2)}, u32[]{:S(2)}) collective-permute-start(bf16[3,256]{1,0:T(4,128)(2,1)S(1)} %copy-done.67), channel_id=1, source_target_pairs={{0,2},{1,3},{2,0},{3,1},{4,6},{5,7},{6,4},{7,5},{8,10},{9,11},{10,... | collective-permute-start | bytes 4616 | tf_op jit(solution)/shard_map/ppermute | solution.py:565
  22.6 96.5 %collective-permute-start.4 = (bf16[256,1024]{1,0:T(8,128)(2,1)}, bf16[256,1024]{1,0:T(8,128)(2,1)}, u32[]{:S(2)}, u32[]{:S(2)}) collective-permute-start(bf16[256,1024]{1,0:T(8,128)(2,1)} %param.27), channel_id=1, source_target_pairs={{0,2},{1,3},{2,0},{3,1},{4,6},{5,7},{6,4},{7,5},{8,10},{9,11},{10,... | collective-permute-start | bytes 1572872 | tf_op jit(solution)/shard_map/ppermute | solution.py:565
  26.1 61.9 %collective-permute-start.2 = (bf16[1024,768]{1,0:T(8,128)(2,1)}, bf16[1024,768]{1,0:T(8,128)(2,1)}, u32[]{:S(2)}, u32[]{:S(2)}) collective-permute-start(bf16[1024,768]{1,0:T(8,128)(2,1)} %copy.140.w_ref), channel_id=1, source_target_pairs={{0,2},{1,3},{2,0},{3,1},{4,6},{5,7},{6,4},{7,5},{8,10},{9,11},{10,... | collective-permute-start | bytes 4718600 | tf_op jit(solution)/shard_map/ppermute | solution.py:565
  45.4 81.6 %all-to-all-start.3 = ((bf16[8,64,1024]{2,1,0:T(8,128)(2,1)}), bf16[8,64,1024]{2,1,0:T(8,128)(2,1)}, u32[]{:S(2)}, u32[]{:S(2)}) async-start(bf16[8,64,1024]{2,1,0:T(8,128)(2,1)} %bitcast.473), calls=%async_computation.3 | async-start | bytes 2097152 | tf_op jit(solution)/shard_map/all_to_all | solution.py:562
  123.6 35.6 %collective-permute-start.8 = (bf16[1024]{0:T(1024)(128)(2,1)S(1)}, bf16[1024]{0:T(1024)(128)(2,1)S(1)}, u32[]{:S(2)}, u32[]{:S(2)}) collective-permute-start(bf16[1024]{0:T(1024)(128)(2,1)S(1)} %copy-done.66), channel_id=1, source_target_pairs={{0,2},{1,3},{2,0},{3,1},{4,6},{5,7},{6,4},{7,5},{8,10},{9,11},{10,... | collective-permute-start | bytes 6152 | tf_op jit(solution)/shard_map/ppermute | solution.py:565
  123.8 48.8 %collective-permute-start.7 = (bf16[1024,1024]{1,0:T(8,128)(2,1)}, bf16[1024,1024]{1,0:T(8,128)(2,1)}, u32[]{:S(2)}, u32[]{:S(2)}) collective-permute-start(bf16[1024,1024]{1,0:T(8,128)(2,1)} %param.29), channel_id=1, source_target_pairs={{0,2},{1,3},{2,0},{3,1},{4,6},{5,7},{6,4},{7,5},{8,10},{9,11},{10,... | collective-permute-start | bytes 6291464 | tf_op jit(solution)/shard_map/ppermute | solution.py:565
  125.6 91.3 %collective-permute-start.9 = (bf16[1024,1024]{1,0:T(8,128)(2,1)}, bf16[1024,1024]{1,0:T(8,128)(2,1)}, u32[]{:S(2)}, u32[]{:S(2)}) collective-permute-start(bf16[1024,1024]{1,0:T(8,128)(2,1)} %param.31), channel_id=1, source_target_pairs={{0,2},{1,3},{2,0},{3,1},{4,6},{5,7},{6,4},{7,5},{8,10},{9,11},{10,... | collective-permute-start | bytes 6291464 | tf_op jit(solution)/shard_map/ppermute | solution.py:565
  129.0 31.8 %collective-permute-start.11 = (bf16[4,128,1024]{2,1,0:T(8,128)(2,1)S(1)}, bf16[4,128,1024]{2,1,0:T(8,128)(2,1)}, u32[]{:S(2)}, u32[]{:S(2)}) collective-permute-start(bf16[4,128,1024]{2,1,0:T(8,128)(2,1)S(1)} %fusion.20), channel_id=1, source_target_pairs={{0,1},{1,0},{2,3},{3,2},{4,5},{5,4},{6,7},{7,6},{8,9},{9,8},{10,11... | collective-permute-start | bytes 3145736 | tf_op jit(solution)/shard_map/ppermute | solution.py:568
  135.3 26.8 %collective-permute-start.6 = (bf16[4,128,1024]{2,1,0:T(8,128)(2,1)}, bf16[4,128,1024]{2,1,0:T(8,128)(2,1)}, u32[]{:S(2)}, u32[]{:S(2)}) collective-permute-start(bf16[4,128,1024]{2,1,0:T(8,128)(2,1)} %add_convert_fusion.2), channel_id=1, source_target_pairs={{0,1},{1,0},{2,3},{3,2},{4,5},{5,4},{6,7},{7,6},{8,9},{9,8},{10,11... | collective-permute-start | bytes 3145736 | tf_op jit(solution)/shard_map/ppermute | solution.py:568
  225.9 104.1 %collective-permute-start.40 = (bf16[1024,1024]{1,0:T(8,128)(2,1)S(1)}, bf16[1024,1024]{1,0:T(8,128)(2,1)S(1)}, u32[]{:S(2)}, u32[]{:S(2)}) collective-permute-start(bf16[1024,1024]{1,0:T(8,128)(2,1)S(1)} %convolution_convert_fusion.1), channel_id=1, source_target_pairs={{0,2},{1,3},{2,0},{3,1},{4,6},{5,7},{6,4},{7,5},{8,10},{9,11},{10,... | collective-permute-start | bytes 6291464 | tf_op jit(solution)/shard_map/ppermute | solution.py:565
  227.7 90.4 %collective-permute-start.47 = (bf16[1024,1024]{1,0:T(8,128)(2,1)S(1)}, bf16[1024,1024]{1,0:T(8,128)(2,1)S(1)}, u32[]{:S(2)}, u32[]{:S(2)}) collective-permute-start(bf16[1024,1024]{1,0:T(8,128)(2,1)S(1)} %convolution_convert_fusion), channel_id=1, source_target_pairs={{0,2},{1,3},{2,0},{3,1},{4,6},{5,7},{6,4},{7,5},{8,10},{9,11},{10,... | collective-permute-start | bytes 6291464 | tf_op jit(solution)/shard_map/ppermute | solution.py:565
  244.5 79.4 %collective-permute-start.12 = (f32[4,128,1024]{2,1,0:T(8,128)S(1)}, f32[4,128,1024]{2,1,0:T(8,128)S(1)}, u32[]{:S(2)}, u32[]{:S(2)}) collective-permute-start(f32[4,128,1024]{2,1,0:T(8,128)S(1)} %slice_bitcast_fusion.2), channel_id=1, source_target_pairs={{0,1},{1,0},{2,3},{3,2},{4,5},{5,4},{6,7},{7,6},{8,9},{9,8},{10,11... | collective-permute-start | bytes 6291464 | tf_op jit(solution)/shard_map/ppermute | solution.py:568
  257.1 69.0 %collective-permute-start.10 = (f32[4,128,1024]{2,1,0:T(8,128)S(1)}, f32[4,128,1024]{2,1,0:T(8,128)S(1)}, u32[]{:S(2)}, u32[]{:S(2)}) collective-permute-start(f32[4,128,1024]{2,1,0:T(8,128)S(1)} %slice_bitcast_fusion.4), channel_id=1, source_target_pairs={{0,1},{1,0},{2,3},{3,2},{4,5},{5,4},{6,7},{7,6},{8,9},{9,8},{10,11... | collective-permute-start | bytes 6291464 | tf_op jit(solution)/shard_map/ppermute | solution.py:568
  322.4 26.4 %collective-permute-start.48 = (bf16[512,1024]{1,0:T(8,128)(2,1)}, bf16[512,1024]{1,0:T(8,128)(2,1)}, u32[]{:S(2)}, u32[]{:S(2)}) collective-permute-start(bf16[512,1024]{1,0:T(8,128)(2,1)} %fusion.23), channel_id=1, source_target_pairs={{0,16},{16,0},{1,17},{17,1},{2,18},{18,2},{3,19},{19,3},{4,20},{20... | collective-permute-start | bytes 3145736 | tf_op jit(solution)/shard_map/ppermute | solution.py:571
  329.5 24.2 %collective-permute-start.13 = (bf16[4,128,1024]{2,1,0:T(8,128)(2,1)S(1)}, bf16[4,128,1024]{2,1,0:T(8,128)(2,1)}, u32[]{:S(2)}, u32[]{:S(2)}) collective-permute-start(bf16[4,128,1024]{2,1,0:T(8,128)(2,1)S(1)} %get-tuple-element.90), channel_id=1, source_target_pairs={{0,1},{1,0},{2,3},{3,2},{4,5},{5,4},{6,7},{7,6},{8,9},{9,8},{10,11... | collective-permute-start | bytes 3145736 | tf_op jit(solution)/shard_map/ppermute | solution.py:568
  335.6 64.8 %collective-permute-start.41 = (bf16[512,1024]{1,0:T(8,128)(2,1)}, bf16[512,1024]{1,0:T(8,128)(2,1)}, u32[]{:S(2)}, u32[]{:S(2)}) collective-permute-start(bf16[512,1024]{1,0:T(8,128)(2,1)} %fusion.22), channel_id=1, source_target_pairs={{0,16},{16,0},{1,17},{17,1},{2,18},{18,2},{3,19},{19,3},{4,20},{20... | collective-permute-start | bytes 3145736 | tf_op jit(solution)/shard_map/ppermute | solution.py:571
  337.1 134.0 %all-to-all-start.2 = ((bf16[8,64,1024]{2,1,0:T(8,128)(2,1)}), bf16[8,64,1024]{2,1,0:T(8,128)(2,1)}, u32[]{:S(2)}, u32[]{:S(2)}) async-start(bf16[8,64,1024]{2,1,0:T(8,128)(2,1)} %bitcast.35), calls=%async_computation.2 | async-start | bytes 2097152 | tf_op jit(solution)/shard_map/all_to_all | solution.py:562
  352.2 79.8 %collective-permute-start.49 = (bf16[256,1024]{1,0:T(8,128)(2,1)}, bf16[256,1024]{1,0:T(8,128)(2,1)}, u32[]{:S(2)}, u32[]{:S(2)}) collective-permute-start(bf16[256,1024]{1,0:T(8,128)(2,1)} %fusion.26), channel_id=1, source_target_pairs={{0,4},{4,0},{8,12},{12,8},{1,5},{5,1},{9,13},{13,9},{2,6},{6,2},{1... | collective-permute-start | bytes 1572872 | tf_op jit(solution)/shard_map/ppermute | solution.py:574
  374.6 34.0 %collective-permute-start.29 = (f32[1792]{0:T(1024)S(1)}, f32[1792]{0:T(1024)S(1)}, u32[]{:S(2)}, u32[]{:S(2)}) collective-permute-start(f32[1792]{0:T(1024)S(1)} %pad_maximum_fusion.23), channel_id=1, source_target_pairs={{0,2},{1,3},{2,0},{3,1},{4,6},{5,7},{6,4},{7,5},{8,10},{9,11},{10,... | collective-permute-start | bytes 21512 | tf_op jit(solution)/shard_map/ppermute | solution.py:565
  404.3 36.5 %collective-permute-start.42 = (bf16[256,1024]{1,0:T(8,128)(2,1)}, bf16[256,1024]{1,0:T(8,128)(2,1)}, u32[]{:S(2)}, u32[]{:S(2)}) collective-permute-start(bf16[256,1024]{1,0:T(8,128)(2,1)} %fusion.25), channel_id=1, source_target_pairs={{0,4},{4,0},{8,12},{12,8},{1,5},{5,1},{9,13},{13,9},{2,6},{6,2},{1... | collective-permute-start | bytes 1572872 | tf_op jit(solution)/shard_map/ppermute | solution.py:574
  404.8 23.9 %collective-permute-start.33 = (bf16[256,1024]{1,0:T(8,128)(2,1)S(1)}, bf16[256,1024]{1,0:T(8,128)(2,1)}, u32[]{:S(2)}, u32[]{:S(2)}) collective-permute-start(bf16[256,1024]{1,0:T(8,128)(2,1)S(1)} %convolution_convert_fusion.3), channel_id=1, source_target_pairs={{0,2},{1,3},{2,0},{3,1},{4,6},{5,7},{6,4},{7,5},{8,10},{9,11},{10,... | collective-permute-start | bytes 1572872 | tf_op jit(solution)/shard_map/ppermute | solution.py:565
  414.8 84.2 %collective-permute-start.20 = (bf16[1024,768]{1,0:T(8,128)(2,1)}, bf16[1024,768]{1,0:T(8,128)(2,1)}, u32[]{:S(2)}, u32[]{:S(2)}) collective-permute-start(bf16[1024,768]{1,0:T(8,128)(2,1)} %convolution_convert_fusion.2), channel_id=1, source_target_pairs={{0,2},{1,3},{2,0},{3,1},{4,6},{5,7},{6,4},{7,5},{8,10},{9,11},{10,... | collective-permute-start | bytes 4718600 | tf_op jit(solution)/shard_map/ppermute | solution.py:565
  427.5 77.3 %collective-permute-start.14 = (f32[4,128,1024]{2,1,0:T(8,128)}, f32[4,128,1024]{2,1,0:T(8,128)}, u32[]{:S(2)}, u32[]{:S(2)}) collective-permute-start(f32[4,128,1024]{2,1,0:T(8,128)} %slice_bitcast_fusion), channel_id=1, source_target_pairs={{0,1},{1,0},{2,3},{3,2},{4,5},{5,4},{6,7},{7,6},{8,9},{9,8},{10,11... | collective-permute-start | bytes 6291464 | tf_op jit(solution)/shard_map/ppermute | solution.py:568
  442.0 26.1 %collective-permute-start.43 = (bf16[128,1024]{1,0:T(8,128)(2,1)S(1)}, bf16[128,1024]{1,0:T(8,128)(2,1)S(1)}, u32[]{:S(2)}, u32[]{:S(2)}) collective-permute-start(bf16[128,1024]{1,0:T(8,128)(2,1)S(1)} %fusion.37), channel_id=1, source_target_pairs={{0,8},{4,12},{8,0},{12,4},{1,9},{5,13},{9,1},{13,5},{2,10},{6,14},... | collective-permute-start | bytes 786440 | tf_op jit(solution)/shard_map/ppermute | solution.py:574
  455.4 26.7 %collective-permute-start.51 = (bf16[128,1024]{1,0:T(8,128)(2,1)S(1)}, bf16[128,1024]{1,0:T(8,128)(2,1)S(1)}, u32[]{:S(2)}, u32[]{:S(2)}) collective-permute-start(bf16[128,1024]{1,0:T(8,128)(2,1)S(1)} %fusion.27), channel_id=1, source_target_pairs={{0,8},{4,12},{8,0},{12,4},{1,9},{5,13},{9,1},{13,5},{2,10},{6,14},... | collective-permute-start | bytes 786440 | tf_op jit(solution)/shard_map/ppermute | solution.py:574
  468.2 23.8 %collective-permute-start.44 = (bf16[128,1024]{1,0:T(8,128)(2,1)S(1)}, bf16[128,1024]{1,0:T(8,128)(2,1)}, u32[]{:S(2)}, u32[]{:S(2)}) collective-permute-start(bf16[128,1024]{1,0:T(8,128)(2,1)S(1)} %fusion.28), channel_id=1, source_target_pairs={{0,8},{4,12},{8,0},{12,4},{1,9},{5,13},{9,1},{13,5},{2,10},{6,14},... | collective-permute-start | bytes 786440 | tf_op jit(solution)/shard_map/ppermute | solution.py:574
  482.3 32.9 %collective-permute-start.52 = (bf16[256,1024]{1,0:T(8,128)(2,1)S(1)}, bf16[256,1024]{1,0:T(8,128)(2,1)}, u32[]{:S(2)}, u32[]{:S(2)}) collective-permute-start(bf16[256,1024]{1,0:T(8,128)(2,1)S(1)} %bitcast.449), channel_id=1, source_target_pairs={{0,4},{4,0},{8,12},{12,8},{1,5},{5,1},{9,13},{13,9},{2,6},{6,2},{1... | collective-permute-start | bytes 1572872 | tf_op jit(solution)/shard_map/ppermute | solution.py:574
  493.8 39.5 %collective-permute-start.45 = (bf16[256,1024]{1,0:T(8,128)(2,1)}, bf16[256,1024]{1,0:T(8,128)(2,1)}, u32[]{:S(2)}, u32[]{:S(2)}) collective-permute-start(bf16[256,1024]{1,0:T(8,128)(2,1)} %bitcast.120), channel_id=1, source_target_pairs={{0,4},{4,0},{8,12},{12,8},{1,5},{5,1},{9,13},{13,9},{2,6},{6,2},{1... | collective-permute-start | bytes 1572872 | tf_op jit(solution)/shard_map/ppermute | solution.py:574
  519.2 53.4 %collective-permute-start.53 = (bf16[512,1024]{1,0:T(8,128)(2,1)S(1)}, bf16[512,1024]{1,0:T(8,128)(2,1)}, u32[]{:S(2)}, u32[]{:S(2)}) collective-permute-start(bf16[512,1024]{1,0:T(8,128)(2,1)S(1)} %bitcast.428), channel_id=1, source_target_pairs={{0,16},{16,0},{1,17},{17,1},{2,18},{18,2},{3,19},{19,3},{4,20},{20... | collective-permute-start | bytes 3145736 | tf_op jit(solution)/shard_map/ppermute | solution.py:571
  535.7 46.4 %collective-permute-start.46 = (bf16[512,1024]{1,0:T(8,128)(2,1)}, bf16[512,1024]{1,0:T(8,128)(2,1)}, u32[]{:S(2)}, u32[]{:S(2)}) collective-permute-start(bf16[512,1024]{1,0:T(8,128)(2,1)} %bitcast.123), channel_id=1, source_target_pairs={{0,16},{16,0},{1,17},{17,1},{2,18},{18,2},{3,19},{19,3},{4,20},{20... | collective-permute-start | bytes 3145736 | tf_op jit(solution)/shard_map/ppermute | solution.py:571
  537.0 60.5 %all-to-all-start.4 = ((bf16[8,64,1024]{2,1,0:T(8,128)(2,1)}), bf16[8,64,1024]{2,1,0:T(8,128)(2,1)}, u32[]{:S(2)}, u32[]{:S(2)}) async-start(bf16[8,64,1024]{2,1,0:T(8,128)(2,1)} %bitcast.51), calls=%async_computation.4 | async-start | bytes 2097152 | tf_op jit(solution)/shard_map/all_to_all | solution.py:562
  (110 other events, 864.3 us)

commit v2 on v1

--- a/solution.py
+++ b/solution.py
@@ -299,47 +299,54 @@
 MIB = 1 << 20
 
 
+def rotary_ladders():
+    first, middle = HD // 4, (HD - HD // 4) // 2
+    bounds = [(0, first), (first, middle), (first + middle, HD - first - middle)]
+    ladders = []
+    for slot, (start, width) in enumerate(bounds):
+        half = width // 2
+        powers = np.arange(half, dtype=np.float32) / np.float32(half)
+        freq = (np.float32(10000.0) ** -powers).astype(np.float32)
+        angle = np.arange(GRID, dtype=np.float32)[:, None] * freq[None, :]
+        cosine, sine = np.cos(angle), np.sin(angle)
+        table = np.zeros((5, GRID, HD), np.float32)
+        up, down = (1, 2) if slot == 0 else (3, 4)
+        table[0, :, start : start + half] = cosine
+        table[0, :, start + half : start + width] = cosine
+        table[up, :, start : start + half] = -sine
+        table[down, :, start + half : start + width] = sine
+        ladders.append(np.tile(table, (1, 1, 2)))
+    return ladders
+
+
+def half_turn(cols):
+    first, middle = HD // 4, (HD - HD // 4) // 2
+    one = np.zeros((HD, HD), np.float32)
+    for start, width in ((0, first), (first, middle), (first + middle, HD - first - middle)):
+        half = width // 2
+        for k in range(half):
+            one[start + half + k, start + k] = -1.0
+            one[start + k, start + half + k] = 1.0
+    return np.kron(np.eye(cols // HD, dtype=np.float32), one)
+
+
 def rotary_tables(core, frames):
+    by_frame, by_row, by_col = rotary_ladders()
     quarter = PATCHES // 4
-    inner = np.arange(quarter)
-    patch = np.zeros((2, 2, 2, quarter), np.int64)
+    steps = quarter // GRID
+    order = np.zeros((2, 2, 2, steps), np.int64)
     for own in range(2):
         for side in range(2):
             for far in range(2):
-                patch[own, side, far] = (2 * far + (own ^ side)) * quarter + inner
-    patch = patch.reshape(2, PATCHES)
-    lane = np.arange(HD)
-    first, middle = HD // 4, (HD - HD // 4) // 2
-    bounds = [(0, first), (first, middle), (first + middle, HD - first - middle)]
-    freq = np.zeros(HD, np.float32)
-    sign_up = np.zeros((2, HD), np.float32)
-    sign_down = np.zeros((2, HD), np.float32)
-    which = np.zeros(HD, np.int64)
-    for slot, (start, width) in enumerate(bounds):
-        half = width // 2
-        ladder = 10000.0 ** (-(np.arange(half, dtype=np.float32) / np.float32(half)))
-        freq[start : start + half] = ladder
-        freq[start + half : start + width] = ladder
-        which[start : start + width] = slot
-        kind = 0 if slot == 0 else 1
-        sign_up[kind, start : start + half] = -1.0
-        sign_down[kind, start + half : start + width] = 1.0
-    del lane
-    frame_pos = jnp.arange(frames, dtype=jnp.float32)[:, None]
-    mine = jnp.asarray(patch)[core]
-    row_pos = (mine // GRID).astype(jnp.float32)[None, :]
-    col_pos = (mine % GRID).astype(jnp.float32)[None, :]
-    shape = (frames, PATCHES)
-    spots = jnp.stack(
-        [jnp.broadcast_to(item, shape) for item in (frame_pos, row_pos, col_pos)]
-    ).reshape(3, frames * PATCHES)
-    angle = spots[which].T * jnp.asarray(freq)[None, :]
-    cosine, sine = jnp.cos(angle), jnp.sin(angle)
-    parts = [cosine]
-    for kind in range(2):
-        parts.append(sine * sign_up[kind])
-        parts.append(sine * sign_down[kind])
-    return jnp.stack([jnp.tile(item, (1, 2)) for item in parts])
+                order[own, side, far] = (2 * far + (own ^ side)) * steps + np.arange(steps)
+    order = order.reshape(2, GRID)
+    rows = jnp.where(core == 0, by_row[:, order[0]], by_row[:, order[1]])
+    full = (
+        jnp.asarray(by_frame)[:, :frames, None, None, :]
+        + rows[:, None, :, None, :]
+        + jnp.asarray(by_col)[:, None, None, :, :]
+    )
+    return full.reshape(5, frames * PATCHES, 2 * HD)
 
 
 def turn(value, tables, sign):
@@ -354,51 +361,489 @@
     return value * tables(0) + (moved if sign > 0 else -moved)
 
 
-def qkv_kernel(rows_ref, w_ref, b_ref, tab_ref, out_ref):
-    step = pl.program_id(0)
-    block = PATCHES
-    for start in range(0, rows_ref.shape[0], block):
-        here = pl.ds(start, block)
-        value = (
-            jnp.dot(rows_ref[here, :], w_ref[...], preferred_element_type=jnp.float32)
-            + b_ref[0].astype(jnp.float32)
-        )
-
-        @pl.when(step < 2)
-        def _():
-            for lane in range(0, value.shape[1], 128):
-                out_ref[0, here, lane : lane + 128] = turn(
-                    value[:, lane : lane + 128], lambda slot: tab_ref[slot, here, :], 1
+ANY = pl.BlockSpec(memory_space=pl.ANY)
+
+
+def qkv_kernel(near_ref, other_ref, w_ref, swing_ref, b_ref, tab_ref, dep_ref, out_ref, turned, bias):
+    del dep_ref
+    cols = out_ref.shape[2]
+
+    @pl.when(pl.program_id(0) == 0)
+    def _():
+        for kind in range(2):
+            lanes = slice(kind * cols, (kind + 1) * cols)
+            turned[:, lanes] = jnp.dot(
+                w_ref[:, lanes], swing_ref[...], preferred_element_type=jnp.float32
+            ).astype(jnp.bfloat16)
+            bias[:, lanes] = jnp.dot(
+                b_ref[:, lanes], swing_ref[...], preferred_element_type=jnp.float32
+            )
+
+    rows = jnp.concatenate([near_ref[0], other_ref[0]], axis=0)
+    for kind in range(3):
+        lanes = slice(kind * cols, (kind + 1) * cols)
+        value = jnp.dot(rows, w_ref[:, lanes], preferred_element_type=jnp.float32)
+        value += b_ref[0, lanes].astype(jnp.float32)[None, :]
+        if kind < 2:
+            moved = jnp.dot(rows, turned[:, lanes], preferred_element_type=jnp.float32)
+            moved += bias[0, lanes][None, :]
+            for lane in range(0, cols, 128):
+                part = slice(lane, lane + 128)
+                out_ref[kind, :, part] = (
+                    value[:, part] * tab_ref[0] + moved[:, part] * tab_ref[1]
                 ).astype(jnp.bfloat16)
-
-        @pl.when(step == 2)
-        def _():
-            out_ref[0, here, :] = value.astype(jnp.bfloat16)
-
-
-def qkv_forward(rows, w, b, tables):
-    count, width = rows.shape
+        else:
+            out_ref[kind] = value.astype(jnp.bfloat16)
+
+
+def qkv_forward(near, other, w, b, two, dep):
+    frames, half, width = near.shape
+    block = 2 * half
+    count = frames * block
     cols = w.shape[1] // 3
+    swing = jnp.asarray(half_turn(cols), jnp.bfloat16)
+    bias = jnp.pad(b.reshape(1, 3 * cols), ((0, 15), (0, 0)))
     return pl.pallas_call(
         qkv_kernel,
-        grid=(3,),
+        grid=(frames,),
         in_specs=[
-            pl.BlockSpec((count, width), lambda i: (0, 0)),
-            pl.BlockSpec((width, cols), lambda i: (0, i)),
-            pl.BlockSpec((1, 1, cols), lambda i: (i, 0, 0)),
-            pl.BlockSpec(tables.shape, lambda i: (0, 0, 0)),
+            pl.BlockSpec((1, half, width), lambda i: (i, 0, 0)),
+            pl.BlockSpec((1, half, width), lambda i: (i, 0, 0)),
+            pl.BlockSpec((width, 3 * cols), lambda i: (0, 0)),
+            pl.BlockSpec((cols, cols), lambda i: (0, 0)),
+            pl.BlockSpec((16, 3 * cols), lambda i: (0, 0)),
+            pl.BlockSpec((2, block, 128), lambda i: (0, i, 0)),
+            ANY,
         ],
-        out_specs=pl.BlockSpec((1, count, cols), lambda i: (i, 0, 0)),
+        out_specs=pl.BlockSpec((3, block, cols), lambda i: (0, i, 0)),
         out_shape=jax.ShapeDtypeStruct((3, count, cols), jnp.bfloat16),
+        scratch_shapes=[
+            pltpu.VMEM((width, 2 * cols), jnp.bfloat16),
+            pltpu.VMEM((16, 2 * cols), jnp.float32),
+        ],
         compiler_params=pltpu.CompilerParams(vmem_limit_bytes=48 * MIB),
         cost_estimate=pl.CostEstimate(
-            flops=2 * count * width * cols * 3, bytes_accessed=12 * MIB, transcendentals=0
+            flops=2 * count * width * cols * 5, bytes_accessed=8 * MIB, transcendentals=0
         ),
         name="qkv_forward",
-    )(rows, w, b[:, None, :], tables)
-
-
-def attend_kernel(frames, qkv_ref, out_ref, lse_ref):
+    )(near, other, w, swing, bias, two, dep)
+
+
+def gate_kernel(value_ref, gate_ref, dep_ref, out_ref):
+    del dep_ref
+    out_ref[...] = (value_ref[...].astype(jnp.float32) * gate_ref[...]).astype(jnp.bfloat16)
+
+
+def gated(value, gate, dep):
+    frames, half, width = value.shape
+    return pl.pallas_call(
+        gate_kernel,
+        grid=(frames,),
+        in_specs=[
+            pl.BlockSpec((1, half, width), lambda i: (i, 0, 0)),
+            pl.BlockSpec((1, 1, width), lambda i: (i, 0, 0)),
+            ANY,
+        ],
+        out_specs=pl.BlockSpec((1, half, width), lambda i: (i, 0, 0)),
+        out_shape=jax.ShapeDtypeStruct(value.shape, jnp.bfloat16),
+        name="gated",
+    )(value, gate, dep)
+
+
+def hidden_kernel(
+    near_ref, other_ref, gn_ref, go_ref, w1_ref, w2_ref, b_ref, *refs
+):
+    act_ref, pre_ref, in_near_ref, in_other_ref, rows_ref, grad_ref, bias_ref, total = refs[-8:]
+    frames, half, width = near_ref.shape
+
+    @pl.when(pl.program_id(0) == 0)
+    def _():
+        for frame in range(frames):
+            for ref, parts in ((rows_ref, (near_ref, other_ref)), (grad_ref, (gn_ref, go_ref))):
+                for side in range(2):
+                    start = (2 * frame + side) * half
+                    ref[start : start + half, :] = parts[side][frame]
+        total[...] = jnp.zeros_like(total)
+
+    root = math.sqrt(2.0 / math.pi)
+    block = 512
+    for start in range(0, rows_ref.shape[0], block):
+        here = slice(start, start + block)
+        pre = jnp.dot(rows_ref[here, :], w1_ref[...], preferred_element_type=jnp.float32)
+        pre += b_ref[...].astype(jnp.float32)
+        back = lax.dot_general(
+            grad_ref[here, :], w2_ref[...], (((1,), (1,)), ((), ())),
+            preferred_element_type=jnp.float32,
+        )
+        square = pre * pre
+        tanh = jnp.tanh(pre * (root + (root * 0.044715) * square))
+        side = 0.5 + 0.5 * tanh
+        act_ref[here, :] = (pre * side).astype(jnp.bfloat16)
+        slope = side + pre * (side * (1.0 - tanh)) * (root + (3 * root * 0.044715) * square)
+        low = (back * slope).astype(jnp.bfloat16)
+        pre_ref[here, :] = low
+        sums = jnp.sum(low.astype(jnp.float32), axis=0, keepdims=True)
+        bias_ref[...] = sums if start == 0 else bias_ref[...] + sums
+        total[here, :] += lax.dot_general(
+            low, w1_ref[...], (((1,), (1,)), ((), ())), preferred_element_type=jnp.float32
+        )
+
+    @pl.when(pl.program_id(0) == pl.num_programs(0) - 1)
+    def _():
+        for frame in range(frames):
+            start = 2 * frame * half
+            in_near_ref[frame] = total[start : start + half, :]
+            in_other_ref[frame] = total[start + half : start + 2 * half, :].astype(jnp.bfloat16)
+
+
+def hidden(near, other, grad_near, grad_other, w1, w2, b, *deps):
+    frames, half, width = near.shape
+    units = w1.shape[1]
+    count = 2 * frames * half
+    step = 256
+    side = pl.BlockSpec((frames, half, width), lambda i: (0, 0, 0))
+    wide = pl.BlockSpec((count, step), lambda i: (0, i))
+    tall = pl.BlockSpec((count, width), lambda i: (0, 0))
+    line = pl.BlockSpec((1, step), lambda i: (0, i))
+    bf16, f32 = jnp.bfloat16, jnp.float32
+    return pl.pallas_call(
+        hidden_kernel,
+        grid=(units // step,),
+        in_specs=[side] * 4
+        + [
+            pl.BlockSpec((width, step), lambda i: (0, i)),
+            pl.BlockSpec((step, width), lambda i: (i, 0)),
+            line,
+        ]
+        + [ANY] * len(deps),
+        out_specs=[wide, wide, side, side, tall, tall, line],
+        out_shape=[
+            jax.ShapeDtypeStruct((count, units), bf16),
+            jax.ShapeDtypeStruct((count, units), bf16),
+            jax.ShapeDtypeStruct((frames, half, width), f32),
+            jax.ShapeDtypeStruct((frames, half, width), bf16),
+            jax.ShapeDtypeStruct((count, width), bf16),
+            jax.ShapeDtypeStruct((count, width), bf16),
+            jax.ShapeDtypeStruct((1, units), f32),
+        ],
+        scratch_shapes=[pltpu.VMEM((count, width), f32)],
+        compiler_params=pltpu.CompilerParams(vmem_limit_bytes=56 * MIB),
+        cost_estimate=pl.CostEstimate(
+            flops=6 * count * width * units,
+            bytes_accessed=20 * MIB,
+            transcendentals=count * units,
+        ),
+        name="hidden",
+    )(near, other, grad_near, grad_other, w1, w2, b.reshape(1, units), *deps)
+
+
+def normal(value):
+    center = value - jnp.mean(value, axis=-1, keepdims=True)
+    root = lax.rsqrt(jnp.mean(center * center, axis=-1, keepdims=True) + epsilon)
+    return center * root, root
+
+
+def normal_back(grad, unit, root):
+    tilt = jnp.mean(grad * unit, axis=-1, keepdims=True)
+    return (grad - jnp.mean(grad, axis=-1, keepdims=True) - unit * tilt) * root
+
+
+def by_frame(kernel, inputs, outs, deps=(), name=None):
+    def spec(shape):
+        if shape[0] == 1:
+            return pl.BlockSpec((1,) + tuple(shape[1:]), lambda i: (0, 0, 0))
+        return pl.BlockSpec((1,) + tuple(shape[1:]), lambda i: (i, 0, 0))
+
+    frames = max(item.shape[0] for item in inputs)
+    ready = len(inputs)
+
+    def run(*refs):
+        kernel(refs[:ready], refs[ready + len(deps) :])
+
+    return pl.pallas_call(
+        run,
+        grid=(frames,),
+        in_specs=[spec(item.shape) for item in inputs] + [ANY] * len(deps),
+        out_specs=[spec(item[0]) for item in outs],
+        out_shape=[jax.ShapeDtypeStruct(*item) for item in outs],
+        compiler_params=pltpu.CompilerParams(vmem_limit_bytes=40 * MIB),
+        name=name,
+    )(*inputs, *deps)
+
+
+def project_kernel(left_ref, w_ref, left_far_ref, w_far_ref, near_ref, other_ref):
+    half = near_ref.shape[1]
+    total = jnp.dot(left_ref[...], w_ref[...], preferred_element_type=jnp.float32)
+    total += jnp.dot(left_far_ref[...], w_far_ref[...], preferred_element_type=jnp.float32)
+    for frame in range(near_ref.shape[0]):
+        start = 2 * half * frame
+        near_ref[frame] = total[start : start + half]
+        other_ref[frame] = total[start + half : start + 2 * half].astype(jnp.bfloat16)
+
+
+def project(left, w, left_far, w_far, frames):
+    count, depth = left.shape
+    width = w.shape[1]
+    half = count // (2 * frames)
+    full = lambda rows, lanes: pl.BlockSpec((rows, lanes), lambda i: (i, 0))
+    same = pl.BlockSpec((depth, width), lambda i: (0, 0))
+    step = 2
+    rows = count * step // frames
+    out = pl.BlockSpec((step, half, width), lambda i: (i, 0, 0))
+    return pl.pallas_call(
+        project_kernel,
+        grid=(frames // step,),
+        in_specs=[full(rows, depth), same, full(rows, depth), same],
+        out_specs=[out, out],
+        out_shape=[
+            jax.ShapeDtypeStruct((frames, half, width), jnp.float32),
+            jax.ShapeDtypeStruct((frames, half, width), jnp.bfloat16),
+        ],
+        compiler_params=pltpu.CompilerParams(vmem_limit_bytes=40 * MIB),
+        name="project",
+    )(left, w, left_far, w_far)
+
+
+SMALL_ROWS = 48
+
+
+def depart_kernel(
+    qkv_ref, qkv_far_ref, out_ref, out_far_ref, tokens_ref,
+    s1_ref, c1_ref, g1_ref, s2_ref, c2_ref, g2_ref,
+    bias_qkv_ref, bias_qkv_far_ref, bias_fc1_ref, bias_out_ref, bias_fc2_ref,
+    qkv_sum, out_sum, tokens_out, gathered,
+    x_away, x_got, z1_away, z1_got, z2_away, z2_got, keep_half,
+    small, small_got, small_low,
+    send, recv, small_send, small_recv, token_send, token_recv,
+):
+    f32, bf16 = jnp.float32, jnp.bfloat16
+    batch, frame, tensor = (lax.axis_index(name) for name in ("batch", "frame", "tensor"))
+    core, far = lax.rem(tensor, 2), lax.div(tensor, 2)
+    low, high = lax.rem(frame, 2), lax.div(frame, 2)
+    other_x = 1 - batch
+    frame_1 = frame + 1 - 2 * low
+    frame_2 = lax.rem(frame + 2, 4)
+    other_core = tensor + 1 - 2 * core
+    place = 2 * frame + far
+
+    def at(b, f, t):
+        return (b, f, t)
+
+    peers = []
+    for flip in range(2):
+        for gap in range(8):
+            if flip or gap:
+                spot = lax.rem(place + gap, 8)
+                b = batch + flip - 2 * flip * batch
+                peers.append((flip, gap, b, spot, lax.div(spot, 2), lax.rem(spot, 2)))
+
+    barrier = pltpu.get_barrier_semaphore()
+    for _, _, b, _, f, y in peers:
+        pl.semaphore_signal(
+            barrier, inc=1, device_id=at(b, f, 2 * y + core), device_id_type=pl.DeviceIdType.MESH
+        )
+    pl.semaphore_signal(
+        barrier, inc=1, device_id=at(batch, frame, other_core),
+        device_id_type=pl.DeviceIdType.MESH,
+    )
+    pl.semaphore_wait(barrier, len(peers) + 1)
+
+    def copy(src, dst, one, two, target):
+        item = pltpu.make_async_remote_copy(
+            src_ref=src, dst_ref=dst, send_sem=one, recv_sem=two,
+            device_id=target, device_id_type=pl.DeviceIdType.MESH,
+        )
+        item.start()
+        return item
+
+    chunks = [(out_ref, out_far_ref, out_sum, 0, out_ref.shape[1])]
+    chunks += [
+        (qkv_ref, qkv_far_ref, qkv_sum, start, qkv_ref.shape[1])
+        for start in range(0, qkv_ref.shape[0], 256)
+    ]
+    piece = 32
+
+    def rows(start, count):
+        return pl.ds(pl.multiple_of(start, piece), count)
+
+    sent = []
+    x_copies = []
+    for k, (own, other, _, base, lanes) in enumerate(chunks):
+        here = rows(base + other_x * 128, 128)
+        x_away[k, :, :lanes] = (own[here, :] + other[here, :].astype(f32)).astype(bf16)
+        x_copies.append(
+            copy(
+                x_away.at[k], x_got.at[k], send.at[k, 0], recv.at[k, 0],
+                at(other_x, frame, tensor),
+            )
+        )
+    mods = (s1_ref, c1_ref, g1_ref, s2_ref, c2_ref, g2_ref)
+    width = small.shape[3]
+    small[...] = jnp.zeros_like(small)
+    for c in range(2):
+        for y in range(2):
+            start = (2 * y + c) * width
+            for j, ref in enumerate(mods):
+                small[c, y, 4 * j : 4 * j + 4, :] = ref[:, 0, start : start + width]
+            for j in range(4):
+                part = slice(j * width, (j + 1) * width)
+                small[c, y, 31 + j : 32 + j, :] = bias_out_ref[:, part]
+                small[c, y, 35 + j : 36 + j, :] = bias_fc2_ref[:, part]
+    core_copy = copy(
+        small.at[1 - core], small_got, small_send.at[15], small_recv.at[15],
+        at(batch, frame, other_core),
+    )
+    token_copies = []
+    for flip, gap, b, spot, f, y in peers:
+        if not flip:
+            token_copies.append(
+                copy(
+                    tokens_ref.at[spot], tokens_out.at[place],
+                    token_send.at[gap - 1], token_recv.at[gap - 1],
+                    at(batch, f, 2 * y + core),
+                )
+            )
+    tokens_out[place] = tokens_ref[place]
+    core_copy.wait()
+    for y in range(2):
+        small_low[y] = (small[core, y] + small_got[y]).astype(bf16)
+    for j in range(3):
+        part = slice(j * width, (j + 1) * width)
+        small_low[far, 24 + j : 25 + j, :] = bias_qkv_ref[:, part].astype(bf16)
+        small_low[1 - far, 24 + j : 25 + j, :] = bias_qkv_far_ref[:, part].astype(bf16)
+    for j in range(4):
+        part = slice(j * width, (j + 1) * width)
+        small_low[far, 27 + j : 28 + j, :] = bias_fc1_ref[:, part].astype(bf16)
+    slot = 8 * batch + place
+    small_copies = []
+    for n, (_, _, b, _, f, y) in enumerate(peers):
+        small_copies.append(
+            copy(
+                small_low.at[y], gathered.at[slot], small_send.at[n], small_recv.at[n],
+                at(b, f, 2 * y + core),
+            )
+        )
+    gathered[slot] = small_low[far]
+
+    z1_copies = []
+    for k, (own, other, _, base, lanes) in enumerate(chunks):
+        x_copies[k].wait_recv()
+        here = rows(base + batch * 128, 128)
+        keep_half[k, :, :lanes] = (
+            own[here, :] + other[here, :].astype(f32) + x_got[k, :, :lanes].astype(f32)
+        )
+        for up in range(2):
+            z1_away[k, up * piece : (up + 1) * piece, :lanes] = keep_half[
+                k, rows((2 * up + 1 - low) * piece, piece), :lanes
+            ].astype(bf16)
+        z1_copies.append(
+            copy(
+                z1_away.at[k], z1_got.at[k], send.at[k, 1], recv.at[k, 1],
+                at(batch, frame_1, tensor),
+            )
+        )
+    z2_copies = []
+    for k, (_, _, _, _, lanes) in enumerate(chunks):
+        z1_copies[k].wait_recv()
+        z2_away[k, :, :lanes] = (
+            keep_half[k, rows(frame_2 * piece, piece), :lanes]
+            + z1_got[k, rows((1 - high) * piece, piece), :lanes].astype(f32)
+        ).astype(bf16)
+        z2_copies.append(
+            copy(
+                z2_away.at[k], z2_got.at[k], send.at[k, 2], recv.at[k, 2],
+                at(batch, frame_2, tensor),
+            )
+        )
+
+    def share(k, total, base, number, owner, target):
+        here = rows(base + batch * 128 + owner * piece, piece)
+        return copy(
+            total.at[here, :], total.at[here, :], send.at[k, number], recv.at[k, number], target
+        )
+
+    shared = []
+    for k, (_, _, total, base, lanes) in enumerate(chunks):
+        z2_copies[k].wait_recv()
+        total[rows(base + batch * 128 + frame * piece, piece), :] = (
+            keep_half[k, rows(frame * piece, piece), :lanes]
+            + z1_got[k, rows(high * piece, piece), :lanes].astype(f32)
+            + z2_got[k, :, :lanes].astype(f32)
+        ).astype(bf16)
+        shared.append(
+            {
+                "z2": share(k, total, base, 3, frame, at(batch, frame_2, tensor)),
+                "z1": share(k, total, base, 4, frame, at(batch, frame_1, tensor)),
+                "x": share(k, total, base, 6, frame, at(other_x, frame, tensor)),
+            }
+        )
+    frame_3 = lax.rem(frame_1 + 2, 4)
+    for k, (_, _, total, base, lanes) in enumerate(chunks):
+        shared[k]["z2"].wait_recv()
+        shared[k]["z1on"] = share(k, total, base, 5, frame_2, at(batch, frame_1, tensor))
+        shared[k]["x2"] = share(k, total, base, 7, frame_2, at(other_x, frame, tensor))
+        shared[k]["z1"].wait_recv()
+        shared[k]["x1"] = share(k, total, base, 8, frame_1, at(other_x, frame, tensor))
+    for k, (_, _, total, base, lanes) in enumerate(chunks):
+        shared[k]["z1on"].wait_recv()
+        shared[k]["x3"] = share(k, total, base, 9, frame_3, at(other_x, frame, tensor))
+    for k in range(len(chunks)):
+        for name in ("x", "x2", "x1", "x3"):
+            shared[k][name].wait_recv()
+    for item in small_copies + token_copies:
+        item.wait()
+    for k in range(len(chunks)):
+        x_copies[k].wait_send()
+        z1_copies[k].wait_send()
+        z2_copies[k].wait_send()
+        for name in ("z2", "z1", "x", "z1on", "x2", "x1", "x3"):
+            shared[k][name].wait_send()
+
+
+def depart(qkv, qkv_far, out, out_far, tokens, mods, biases):
+    f32, bf16 = jnp.float32, jnp.bfloat16
+    chunks = 1 + qkv.shape[0] // 256
+    lanes = max(qkv.shape[1], out.shape[1])
+    cols = qkv.shape[1] // 3
+    vmem = pl.BlockSpec(memory_space=pltpu.VMEM)
+    inputs = [qkv, qkv_far, out, out_far, tokens, *mods, *biases]
+    return pl.pallas_call(
+        depart_kernel,
+        in_specs=[vmem] * len(inputs),
+        out_specs=[vmem] * 4,
+        out_shape=[
+            jax.ShapeDtypeStruct(qkv.shape, bf16),
+            jax.ShapeDtypeStruct(out.shape, bf16),
+            jax.ShapeDtypeStruct(tokens.shape, bf16),
+            jax.ShapeDtypeStruct((16, SMALL_ROWS, cols), bf16),
+        ],
+        scratch_shapes=[
+            pltpu.VMEM((chunks, 128, lanes), bf16),
+            pltpu.VMEM((chunks, 128, lanes), bf16),
+            pltpu.VMEM((chunks, 64, lanes), bf16),
+            pltpu.VMEM((chunks, 64, lanes), bf16),
+            pltpu.VMEM((chunks, 32, lanes), bf16),
+            pltpu.VMEM((chunks, 32, lanes), bf16),
+            pltpu.VMEM((chunks, 128, lanes), f32),
+            pltpu.VMEM((2, 2, SMALL_ROWS, cols), f32),
+            pltpu.VMEM((2, SMALL_ROWS, cols), f32),
+            pltpu.VMEM((2, SMALL_ROWS, cols), bf16),
+            pltpu.SemaphoreType.DMA((chunks, 10)),
+            pltpu.SemaphoreType.DMA((chunks, 10)),
+            pltpu.SemaphoreType.DMA((16,)),
+            pltpu.SemaphoreType.DMA((16,)),
+            pltpu.SemaphoreType.DMA((7,)),
+            pltpu.SemaphoreType.DMA((7,)),
+        ],
+        compiler_params=pltpu.CompilerParams(
+            collective_id=1, has_side_effects=True, vmem_limit_bytes=50 * MIB
+        ),
+        name="depart",
+    )(*inputs)
+
+
+def attend_kernel(frames, qkv_ref, dep_ref, out_ref, lse_ref):
+    del dep_ref
     lanes = qkv_ref.shape[2]
     low_lane = lax.broadcasted_iota(jnp.int32, (PATCHES, lanes), 1) < HD
     for frame in range(frames):
@@ -426,13 +871,13 @@
         lse_ref[0, here, :] = jnp.concatenate(sums, axis=1)
 
 
-def attend(qkv, frames):
+def attend(qkv, frames, dep):
     _, count, cols = qkv.shape
     pairs = cols // 128
     return pl.pallas_call(
         partial(attend_kernel, frames),
         grid=(pairs,),
-        in_specs=[pl.BlockSpec((3, count, 128), lambda i: (0, 0, i))],
+        in_specs=[pl.BlockSpec((3, count, 128), lambda i: (0, 0, i)), ANY],
         out_specs=[
             pl.BlockSpec((count, 128), lambda i: (0, i)),
             pl.BlockSpec((1, count, 2), lambda i: (i, 0, 0)),
@@ -446,10 +891,13 @@
             flops=12_000_000_000, bytes_accessed=4 * MIB, transcendentals=2_600_000
         ),
         name="attend",
-    )(qkv)
-
-
-def attend_back_kernel(frames, qkv_ref, grad_ref, lse_ref, tab_ref, out_ref, dk_ref, dv_ref):
+    )(qkv, dep)
+
+
+def attend_back_kernel(
+    frames, qkv_ref, grad_ref, lse_ref, tab_ref, *refs
+):
+    out_ref, dk_ref, dv_ref = refs[-3:]
     lanes = qkv_ref.shape[2]
     low_lane = lax.broadcasted_iota(jnp.int32, (PATCHES, lanes), 1) < HD
     scale = 1.0 / math.sqrt(HD)
@@ -500,7 +948,7 @@
     out_ref[2] = dv_ref[...].astype(jnp.bfloat16)
 
 
-def attend_back(qkv, grad, lse, tables, frames):
+def attend_back(qkv, grad, lse, tables, frames, *deps):
     _, count, cols = qkv.shape
     pairs = cols // 128
     return pl.pallas_call(
@@ -511,7 +959,8 @@
             pl.BlockSpec((count, 128), lambda i: (0, i)),
             pl.BlockSpec((1, count, 2), lambda i: (i, 0, 0)),
             pl.BlockSpec(tables.shape, lambda i: (0, 0, 0)),
-        ],
+        ]
+        + [ANY] * len(deps),
         out_specs=pl.BlockSpec((3, count, 128), lambda i: (0, 0, i)),
         out_shape=jax.ShapeDtypeStruct((3, count, cols), jnp.bfloat16),
         scratch_shapes=[
@@ -523,7 +972,7 @@
             flops=24_000_000_000, bytes_accessed=6 * MIB, transcendentals=2_600_000
         ),
         name="attend_back",
-    )(qkv, grad, lse, tables)
+    )(qkv, grad, lse, tables, *deps)
 
 
 def fast_body(
@@ -583,9 +1032,11 @@
 
     def sum_cores(term):
         split = term.reshape(frames, 2, rows_own // frames, width)
-        return split[:, 0] + swap_core(split[:, 1])
-
-    tables = rotary_tables(core, frames)
+        return split[:, 0] + swap_core(split[:, 1].astype(bf16)).astype(f32)
+
+    noise_all = lax.all_to_all(
+        jnp.broadcast_to(noise_level[None, :, 0], (2 * frames, clips)), ("batch", "frame"), 0, 0
+    ).reshape(2, frames, frames, 2)
     condition = jax.nn.silu(embedding(noise_level, width)).astype(bf16)
     mod_part = jnp.einsum(
         "cfd,dke->cfke", condition, w_ada, preferred_element_type=f32
@@ -595,104 +1046,126 @@
     modulation = ordered(mod_own, swap_core(mod_own), core)
     modulation = modulation.transpose(1, 3, 2, 0, 4).reshape(frames, 6, width)
     pieces = [modulation[:, slot : slot + 1, :] for slot in range(6)]
+    tables = rotary_tables(core, frames)
+    two = jnp.stack([tables[0], (tables[2] + tables[4]) - (tables[1] + tables[3])])
     w_qkv_own = w_qkv.reshape(width, 3 * cols)
     w_qkv_far = swap_y(w_qkv_own)
     b_qkv_far = swap_y(b_qkv)
-    b_fc1_far = swap_y(b_fc1)
     w_out_far = swap_y(w_out)
-    w_fc1_far = swap_y(w_fc1)
-    w_fc2_far = swap_y(w_fc2)
-    cot_own = to_clip(cotangent[:, 0]).reshape(frames, 2 * quarter, width)
-
-    resid_in = tokens_own.astype(f32)
-    attn_val, ln_one_back = jax.vjp(modulate, resid_in, pieces[0], pieces[1])
-    attn_rows = both_cores(attn_val.astype(bf16))
-    qkv_own = qkv_forward(attn_rows, w_qkv_own, b_qkv, tables)
-    mixed_own, lse_own = attend(qkv_own, frames)
-    qkv_far = qkv_forward(attn_rows, w_qkv_far, b_qkv_far, tables)
-    mixed_far, lse_far = attend(qkv_far, frames)
-    attn_term = jnp.dot(mixed_own, w_out, preferred_element_type=f32) + jnp.dot(
-        mixed_far, w_out_far, preferred_element_type=f32
-    )
-    attn_branch = sum_cores(attn_term) + b_out.astype(f32)
-    resid_one = resid_in + pieces[2] * attn_branch
-    mlp_val, ln_two_back = jax.vjp(modulate, resid_one, pieces[3], pieces[4])
-    mlp_rows = both_cores(mlp_val.astype(bf16))
-
-    upstream = cot_own.astype(f32)
-    mlp_grad = (pieces[5] * upstream).astype(bf16)
-    mlp_grad_rows = both_cores(mlp_grad)
-
-    def hidden(w_one, b_one, w_two):
-        pre_act = jnp.dot(mlp_rows, w_one, preferred_element_type=f32) + b_one.astype(f32)
-        act_val, gelu_back = jax.vjp(partial(jax.nn.gelu, approximate=True), pre_act)
-        activated = act_val.astype(bf16)
-        mlp_term = jnp.dot(activated, w_two, preferred_element_type=f32)
-        act_grad = lax.dot_general(
-            mlp_grad_rows, w_two, (((1,), (1,)), ((), ())), preferred_element_type=f32
-        )
-        pre_grad = gelu_back(act_grad)[0].astype(bf16)
-        in_term = lax.dot_general(
-            pre_grad, w_one, (((1,), (1,)), ((), ())), preferred_element_type=f32
-        )
-        two_grad = lax.dot_general(
-            activated, mlp_grad_rows, (((0,), (0,)), ((), ())), preferred_element_type=f32
-        )
-        one_grad = lax.dot_general(
-            mlp_rows, pre_grad, (((0,), (0,)), ((), ())), preferred_element_type=f32
-        )
-        bias_grad = jnp.sum(pre_grad.astype(f32), axis=0)
-        return mlp_term, in_term, one_grad, two_grad, bias_grad
-
-    term_own, in_own, fc1_own, fc2_own, fc1_bias_own = hidden(w_fc1, b_fc1, w_fc2)
-    term_far, in_far, fc1_far, fc2_far, fc1_bias_far = hidden(w_fc1_far, b_fc1_far, w_fc2_far)
-    mlp_in_grad = sum_cores(in_own + in_far)
-    mlp_branch = sum_cores(term_own + term_far) + b_fc2.astype(f32)
-    output_own = (resid_one + pieces[5] * mlp_branch).astype(bf16)
-    gate_two_grad = jnp.sum(upstream * mlp_branch, axis=1, keepdims=True)
+
+    shape = (frames, 2 * quarter, width)
+    line = (frames, 1, width)
+
+    def first_norm(ins, outs):
+        unit, _ = normal(ins[0][0].astype(f32))
+        outs[0][0] = (unit * (1.0 + ins[2][0]) + ins[1][0]).astype(bf16)
+
+    (attn_in,) = by_frame(
+        first_norm, [tokens_own, pieces[0], pieces[1]], [(shape, bf16)], name="first_norm"
+    )
+    attn_in_other = swap_core(attn_in)
+    attn_rows = jnp.concatenate([attn_in, attn_in_other], axis=1).reshape(count, width)
+    qkv_own = qkv_forward(attn_in, attn_in_other, w_qkv_own, b_qkv, two, noise_level)
+    mixed_own, lse_own = attend(qkv_own, frames, noise_level)
+    qkv_far = qkv_forward(attn_in, attn_in_other, w_qkv_far, b_qkv_far, two, mixed_own)
+
+    cot_own = to_clip(cotangent[:, 0]).reshape(shape)
+    mlp_grad = gated(cot_own, pieces[5], qkv_far)
+    mixed_far, lse_far = attend(qkv_far, frames, mlp_grad)
+    mlp_grad_far = swap_y(mlp_grad)
     fc2_bias_part = jnp.sum(mlp_grad.astype(f32), axis=(0, 1))
 
-    def over_xz(total):
-        rows, lanes = total.shape
-        low_bit, high_bit = frame_now % 2, frame_now // 2
-
-        def halve(item, place, send):
-            split = item.reshape(2, item.shape[0] // 2, lanes)
-            keep = lax.dynamic_index_in_dim(split, place, 0, False)
-            away = lax.dynamic_index_in_dim(split, 1 - place, 0, False)
-            return keep + send(away.astype(bf16)).astype(f32)
-
-        def join(item, place, send):
-            return ordered(item, send(item), place).reshape(2 * item.shape[0], lanes)
-
-        part = halve(total, batch_now, swap_x)
-        part = halve(part, low_bit, lambda item: swap_z(item, 1))
-        part = halve(part, high_bit, lambda item: swap_z(item, 2)).astype(bf16)
-        part = join(part, high_bit, lambda item: swap_z(item, 2))
-        part = join(part, low_bit, lambda item: swap_z(item, 1))
-        return join(part, batch_now, swap_x).astype(f32)
-
-    def reduced(own, other):
-        return over_xz(own + swap_y(other.astype(bf16)).astype(f32))
-
-    fc2_grad = reduced(fc2_own, fc2_far)
-    fc1_grad = reduced(fc1_own, fc1_far)
-
-    resid_part, shift_two_grad, scale_two_grad = ln_two_back(mlp_in_grad)
-    resid_grad = upstream + resid_part
-    attn_grad = (pieces[2] * resid_grad).astype(bf16)
-    gate_one_grad = jnp.sum(resid_grad * attn_branch, axis=1, keepdims=True)
-    out_bias_part = jnp.sum(attn_grad.astype(f32), axis=(0, 1))
+    term_near, term_other = project(mixed_own, w_out, mixed_far, w_out_far, frames)
+
+    def second_norm(ins, outs):
+        near, other, bias, value, gate, shift, scale = (item[0].astype(f32) for item in ins)
+        branch = near + other + bias
+        resid = value + gate * branch
+        unit, _ = normal(resid)
+        outs[0][0] = branch
+        outs[1][0] = resid
+        outs[2][0] = (unit * (1.0 + scale) + shift).astype(bf16)
+
+    attn_branch, resid_one, mlp_in = by_frame(
+        second_norm,
+        [term_near, swap_core(term_other), b_out.reshape(1, 1, width), tokens_own]
+        + [pieces[2], pieces[3], pieces[4]],
+        [(shape, f32), (shape, f32), (shape, bf16)],
+        name="second_norm",
+    )
+    mlp_in_far = swap_y(mlp_in)
+
+    act_near, pre_near, in_near, in_near_away, rows_near, grad_near, bias_near = hidden(
+        mlp_in, swap_core(mlp_in), mlp_grad, swap_core(mlp_grad), w_fc1, w_fc2, b_fc1
+    )
+    act_far, pre_far, in_far, in_far_away, rows_far, grad_far, bias_far = hidden(
+        mlp_in_far, swap_core(mlp_in_far), mlp_grad_far, swap_core(mlp_grad_far),
+        w_fc1, w_fc2, b_fc1, act_near,
+    )
+    in_back = swap_y((in_far + swap_core(in_far_away).astype(f32)).astype(bf16))
+    fc1_bias_own = (bias_near + bias_far)[0]
+
+    def outer(left_near, right_near, left_far, right_far):
+        dims = (((0,), (0,)), ((), ()))
+        return lax.dot_general(
+            left_near, right_near, dims, preferred_element_type=f32
+        ) + lax.dot_general(left_far, right_far, dims, preferred_element_type=f32)
+
+    fc2_own = outer(act_near, grad_near, act_far, grad_far).astype(bf16)
+    fc1_own = outer(rows_near, pre_near, rows_far, pre_far).astype(bf16)
+    fc2_sum, fc1_sum = lax.psum((fc2_own, fc1_own), ("batch", "frame"))
+
+    def branch_parts(activated):
+        term = jnp.dot(activated, w_fc2, preferred_element_type=f32)
+        term = term.reshape(frames, 2, 2 * quarter, width)
+        return term[:, 0], swap_core(term[:, 1].astype(bf16))
+
+    far_near, far_other = branch_parts(act_far)
+    branch_back = swap_y((far_near + far_other.astype(f32)).astype(bf16))
+    branch_near, branch_other = branch_parts(act_near)
+
+    def second_back(ins, outs):
+        near, other, back, resid, cot, branch, gate, scale = (item[0].astype(f32) for item in ins)
+        grad = near + other + back
+        unit, root = normal(resid)
+        outs[0][0] = jnp.sum(grad, axis=0, keepdims=True)
+        outs[1][0] = jnp.sum(grad * unit, axis=0, keepdims=True)
+        through = cot + normal_back(grad * (1.0 + scale), unit, root)
+        outs[2][0] = through
+        low = (gate * through).astype(bf16)
+        outs[3][0] = low
+        outs[4][0] = jnp.sum(through * branch, axis=0, keepdims=True)
+        outs[5][0] = jnp.sum(low.astype(f32), axis=0, keepdims=True)
+
+    shift_two_grad, scale_two_grad, resid_grad, attn_grad, gate_one_grad, out_bias = by_frame(
+        second_back,
+        [in_near, swap_core(in_near_away), in_back, resid_one, cot_own, attn_branch]
+        + [pieces[2], pieces[4]],
+        [(line, f32), (line, f32), (shape, f32), (shape, bf16), (line, f32), (line, f32)],
+        [fc1_own, fc2_own, far_near, branch_near],
+        name="second_back",
+    )
+    out_bias_part = jnp.sum(out_bias, axis=(0, 1))
     attn_grad_rows = both_cores(attn_grad)
 
-    def heads_back(w, qkv, mixed, lse, w_in):
-        mixed_grad = lax.dot_general(
+    def last_gate(ins, outs):
+        near, other, back, bias, resid, gate, cot = (item[0].astype(f32) for item in ins)
+        branch = near + other + back + bias
+        outs[0][0] = (resid + gate * branch).astype(bf16)
+        outs[1][0] = jnp.sum(cot * branch, axis=0, keepdims=True)
+
+    def back_mixed(w):
+        return lax.dot_general(
             attn_grad_rows, w, (((1,), (1,)), ((), ())), preferred_element_type=f32
         ).astype(bf16)
-        out_grad = lax.dot_general(
+
+    def out_outer(mixed):
+        return lax.dot_general(
             mixed, attn_grad_rows, (((0,), (0,)), ((), ())), preferred_element_type=f32
         )
-        back = attend_back(qkv, mixed_grad, lse, tables, frames)
+
+    def heads_back(qkv, mixed_grad, lse, w_in, *deps):
+        back = attend_back(qkv, mixed_grad, lse, tables, frames, *deps)
         back = back.transpose(1, 0, 2).reshape(count, 3 * cols)
         qkv_grad = lax.dot_general(
             attn_rows, back, (((0,), (0,)), ((), ())), preferred_element_type=f32
@@ -700,83 +1173,76 @@
         in_term = lax.dot_general(
             back, w_in, (((1,), (1,)), ((), ())), preferred_element_type=f32
         )
-        return out_grad, qkv_grad, jnp.sum(back.astype(f32), axis=0), in_term
-
-    out_far, qkv_grad_far, qkv_bias_far, attn_in_far = heads_back(
-        w_out_far, qkv_far, mixed_far, lse_far, w_qkv_far
-    )
-    out_own, qkv_grad_own, qkv_bias_own, attn_in_own = heads_back(
-        w_out, qkv_own, mixed_own, lse_own, w_qkv_own
-    )
-    out_grad = reduced(out_own, out_far)
-    qkv_grad = reduced(qkv_grad_own, qkv_grad_far).reshape(width, 3, cols)
-    attn_in_grad = sum_cores(attn_in_own + attn_in_far)
-    input_part, shift_one_grad, scale_one_grad = ln_one_back(attn_in_grad)
-    tokens_grad_own = resid_grad + input_part
-    tokens_grad = to_clip(tokens_grad_own.astype(bf16).reshape(clips, quarter, width))
+        return back, qkv_grad, jnp.sum(back.astype(f32), axis=0), in_term
+
+    out_arrived = swap_y(out_outer(mixed_far).astype(bf16))
+    mixed_grad_far = back_mixed(w_out_far)
+    mixed_grad_own = back_mixed(w_out)
+    back_far, qkv_grad_far, qkv_bias_far, attn_in_far = heads_back(
+        qkv_far, mixed_grad_far, lse_far, w_qkv_far, mixed_grad_own
+    )
+    qkv_low_far = qkv_grad_far.astype(bf16)
+    qkv_arrived = swap_y(qkv_low_far)
+    output_own, gate_two_grad = by_frame(
+        last_gate,
+        [branch_near, branch_other, branch_back, b_fc2.reshape(1, 1, width), resid_one]
+        + [pieces[5], cot_own],
+        [(shape, bf16), (line, f32)],
+        [back_far],
+        name="last_gate",
+    )
     output = to_clip(output_own.reshape(clips, quarter, width))
-
-    mod_grad = jnp.concatenate(
-        [
-            shift_one_grad,
-            scale_one_grad,
-            gate_one_grad,
-            shift_two_grad,
-            scale_two_grad,
-            gate_two_grad,
-        ],
-        axis=1,
-    )
-    mod_grad = mod_grad + swap_core(mod_grad)
-    mod_cols = mod_grad.reshape(frames, 6, 4, cols)
-    mod_mine = lax.dynamic_index_in_dim(mod_cols, tensor_now, 2, False)
-    mod_away = lax.dynamic_index_in_dim(mod_cols, jnp.bitwise_xor(tensor_now, 2), 2, False)
-    shared = jnp.concatenate([out_bias_part, fc2_bias_part])
-    shared = shared + swap_core(shared)
-    shared = shared + swap_y(shared)
-    local = jnp.concatenate([fc1_bias_own, qkv_bias_own])
-    away = jnp.concatenate([fc1_bias_far, qkv_bias_far])
-    small = jnp.concatenate([shared, local + swap_y(away)])
-    gathered = jnp.stack([mod_mine, swap_y(mod_away)])
-    gathered = jnp.stack([gathered, swap_x(gathered)])
-    gathered = jnp.stack([gathered, swap_z(gathered, 1)])
-    gathered = jnp.stack([gathered, swap_z(gathered, 2)])
-    small = small + swap_x(small)
-    small = small + swap_z(small, 1)
-    small = small + swap_z(small, 2)
-    flips = jnp.arange(32 // 2)
-    origin = (
-        frame_now * 4 + batch_now * 2 + far
-    )
-    gathered = gathered.reshape(16, frames, 6, cols)[jnp.bitwise_xor(flips, origin)]
-    noise_all = lax.all_gather(noise_level, ("batch", "frame"))[..., 0]
-    noise_all = noise_all.reshape(2, frames, frames, 2)
-    noise_all = noise_all.transpose(2, 0, 3, 1).reshape(16 * frames)
+    back_own, qkv_grad_own, qkv_bias_own, attn_in_own = heads_back(
+        qkv_own, mixed_grad_own, lse_own, w_qkv_own, qkv_low_far, output_own
+    )
+    in_term = (attn_in_own + attn_in_far).reshape(frames, 2, 2 * quarter, width)
+
+    def first_back(ins, outs):
+        near, other, value, above, scale = (item[0].astype(f32) for item in ins)
+        grad = near + other
+        unit, root = normal(value)
+        outs[0][0] = jnp.sum(grad, axis=0, keepdims=True)
+        outs[1][0] = jnp.sum(grad * unit, axis=0, keepdims=True)
+        outs[2][0] = (above + normal_back(grad * (1.0 + scale), unit, root)).astype(bf16)
+
+    shift_one_grad, scale_one_grad, tokens_low = by_frame(
+        first_back,
+        [in_term[:, 0], swap_core(in_term[:, 1].astype(bf16)), tokens_own, resid_grad, pieces[1]],
+        [(line, f32), (line, f32), (shape, bf16)],
+        name="first_back",
+    )
+    mods = [shift_one_grad, scale_one_grad, gate_one_grad]
+    mods += [shift_two_grad, scale_two_grad, gate_two_grad]
+    biases = [qkv_bias_own, qkv_bias_far, fc1_bias_own, out_bias_part, fc2_bias_part]
+    qkv_sum, out_sum, tokens_grad, gathered = depart(
+        qkv_grad_own, qkv_arrived, out_outer(mixed_own), out_arrived,
+        tokens_low.reshape(clips, quarter, width), mods, [item[None, :] for item in biases],
+    )
+    noise_all = noise_all.transpose(0, 2, 3, 1).reshape(16 * frames)
     condition_all = jax.nn.silu(embedding(noise_all, width)).astype(bf16)
-    mod_flat = gathered.reshape(16 * frames, 6 * cols)
+    mod_all = gathered[:, : 6 * frames].reshape(16, 6, frames, cols).transpose(0, 2, 1, 3)
     ada_grad = lax.dot_general(
-        condition_all.astype(f32),
-        mod_flat,
+        condition_all,
+        mod_all.reshape(16 * frames, 6 * cols),
         (((0,), (0,)), ((), ())),
-        precision=lax.Precision.HIGHEST,
         preferred_element_type=f32,
     ).reshape(width, 6, cols)
-    ada_bias_grad = jnp.sum(gathered, axis=(0, 1))
-    hidden_cols = fc1_bias_own.shape[0]
-    fc1_end = 2 * width + hidden_cols
+    rows_sum = jnp.sum(gathered.astype(f32), axis=0)
+    ada_bias_grad = jnp.sum(rows_sum[: 6 * frames].reshape(6, frames, cols), axis=1)
+    hidden_rows = fc1_bias_own.shape[0] // cols
     return (
         output[:, None],
         tokens_grad.astype(f32)[:, None],
         ada_grad,
         ada_bias_grad,
-        qkv_grad,
-        small[fc1_end:].reshape(3, cols),
-        out_grad,
-        small[:width],
-        fc1_grad,
-        small[2 * width : fc1_end],
-        fc2_grad,
-        small[width : 2 * width],
+        qkv_sum.astype(f32).reshape(width, 3, cols),
+        rows_sum[24:27],
+        out_sum.astype(f32),
+        rows_sum[31:35].reshape(width),
+        fc1_sum.astype(f32),
+        rows_sum[27 : 27 + hidden_rows].reshape(4 * cols),
+        fc2_sum.astype(f32),
+        rows_sum[35:39].reshape(width),
     )
 
 

time: 627 us -> 524 us (0.84)
  Pallas kernels: 67.4 us -> 246 us
  waiting for transfers between devices: 246 us -> 70 us
  other arithmetic: 62.5 us -> 25.1 us
  starting transfers between devices: 63 us -> 28.4 us
  matrix products: 85 us -> 52.4 us
  blocking collectives: 35.4 us -> 14 us
  between operations: 3.59 us -> 15.4 us
  local copies, waits for them, and re-layouts: 60 us -> 68.7 us
    pallas_call x2 -> x12, Pallas kernels: 20.6 us -> 199 us  [the longest x1 134 us: depart(): pl.pallas_call(depart_kernel, in_specs=[vmem] * len(inputs), out_specs=[v...]
    ppermute x30 -> x0, waiting for transfers between devices: 113 us -> none  [the longest x20 81 us: swap_z(): return lax.ppermute(item, 'frame', [(f, f ^ bit) for f in range(frames)])]
    ppermute x13 -> x9, waiting for transfers between devices: 115 us -> 45.2 us  [swap_y(): return lax.ppermute(item, 'tensor', [(t, t ^ 2) for t in range(4)])]
    dot_general x19 -> x11, matrix products: 69.4 us -> 35.9 us  [the longest x2 8.9 us: outer(): lax.dot_general(left_near, right_near, dims, preferred_element_type=f32)]
    ppermute x30 -> x0, starting transfers between devices: 29.3 us -> none  [the longest x20 17.9 us: swap_z(): return lax.ppermute(item, 'frame', [(f, f ^ bit) for f in range(frames)])]
    unnamed x1 -> x0, blocking collectives: 21.5 us -> none
    reduce_sum x13 -> x5, other arithmetic: 15.3 us -> 1.19 us  [the longest x1 0.62 us: fast_body(): jnp.sum(rows_sum[:6 * frames].reshape(6, frames, cols), axis=1)]
    unnamed x186 -> x190, local copies, waits for them, and re-layouts: 28.1 us -> 41.3 us
  transfers between devices with their start and end apart: 58 -> 27, of which waited for: 23 -> 6; matrix products, arithmetic and copies ran while one was open for 27% -> 20% of each run, Pallas kernels for 11% -> 47%
where the time goes in v2:
time: 524 us; the launch traced here: 520 us
  Pallas kernels  246 us (47%)
  waiting for transfers between devices  70 us (13%)
  local copies, waits for them, and re-layouts  68.7 us (13%)
  matrix products  52.4 us (10%)
  starting transfers between devices  28.4 us (5%)
  other arithmetic  25.1 us (5%)
  between operations  15.4 us (3%)
  blocking collectives  14 us (3%)
    pallas_call x1, Pallas kernels, depart(): pl.pallas_call(depart_kernel, in_specs=[vmem] * len(inputs), out_specs=[v...  134 us
    ppermute x9, waiting for transfers between devices, swap_y(): return lax.ppermute(item, 'tensor', [(t, t ^ 2) for t in range(4)])  45.2 us
    unnamed x190, local copies, waits for them, and re-layouts  41.3 us
    pallas_call x2, Pallas kernels, hidden(): pl.pallas_call(hidden_kernel, grid=(units // step,), in_specs=[side] * 4...  32.7 us
    pallas_call x2, Pallas kernels, attend_back(): pl.pallas_call(partial(attend_back_kernel, frames), grid=(pairs,), in_spe...  29.7 us
    pallas_call x2, Pallas kernels, attend(): pl.pallas_call(partial(attend_kernel, frames), grid=(pairs,), in_specs=[p...  17.4 us
    all_to_all x3, waiting for transfers between devices, to_clip(): lax.all_to_all(item, ('frame', 'tensor'), 0, 0, axis_index_groups=groups)  17 us
    pallas_call x5, Pallas kernels, by_frame(): pl.pallas_call(run, grid=(frames,), in_specs=[spec(item.shape) for item i...  14.8 us
  transfers between devices with their start and end apart: 27, of which 6 were waited for; matrix products, arithmetic and copies ran while one was open for 20% of the time, Pallas kernels for 47%

profile of v2, /device:TPU:0, one launch (start us, length us, event | category | flops | bytes accessed | tf_op | source)
XLA Modules:
  0.0 520.4 jit_solution(15130123373718578126)
XLA Ops:
  9.6 14.0 %all_to_all.26 = f32[8,6,256]{2,1,0:T(8,128)S(1)} all-to-all(f32[8,6,256]{2,1,0:T(8,128)S(1)} %copy.101), channel_id=1, replica_groups={{0,2,4,6,8,10,12,14},{1,3,5,7,9,11,13,15},{16,18,20,22,24,26,28,30},{17..., dimensions={0} | all-to-all | bytes 98304 | tf_op jit(solution)/shard_map/all_to_all | solution.py:1011
  23.6 3.6 all-to-all-start
  35.0 17.0 %all-to-all-done = bf16[8,64,1024]{2,1,0:T(8,128)(2,1)S(1)} async-done(((bf16[8,64,1024]{2,1,0:T(8,128)(2,1)}), bf16[8,64,1024]{2,1,0:T(8,128)(2,1)S(1)}, u32[]{:S(2)}, u32[]{:S(2)}) %all-to-all-start) | async-done | bytes 1048608 | tf_op jit(solution)/shard_map/all_to_all | solution.py:1011
  52.0 3.9 all-to-all-start.2
  60.1 22.5 %collective-permute-done.3 = bf16[3,256]{1,0:T(4,128)(2,1)S(1)} collective-permute-done((bf16[3,256]{1,0:T(4,128)(2,1)S(1)}, bf16[3,256]{1,0:T(4,128)(2,1)S(1)}, u32[]{:S(2)}, u32[]{:S(2)}) %collective-permute-start.3) | collective-permute-done | bytes 1568 | tf_op jit(solution)/shard_map/ppermute | solution.py:1014
  84.5 5.6 %qkv_forward.2.qkv_ref = bf16[3,1024,256]{2,1,0:T(8,128)(2,1)S(1)} custom-call(bf16[4,128,1024]{2,1,0:T(8,128)(2,1)S(1)} %first_norm.1.near_ref, bf16[4,128,1024]{2,1,0:T(8,128)(2,1)} %collective-permute-done.1.other_ref, bf16[1024,768]{1,0:T(8,128)(2,1)} %copy.109.w_ref, bf16[256,256]{1,0:T(8,128)(2,1)S(1)} %copy-done.34, bf16[16,768]{1,0:T(8,128)(2,1)S(1)} %pad.7.b_ref, ...), custom_call_target="tpu_custom_call" | custom-call | flops 2684354560 | bytes 8388608 | tf_op jit(solution)/shard_map/qkv_forward/pallas_call | solution.py:406
  90.1 8.7 %attend.2 = (bf16[1024,256]{1,0:T(8,128)(2,1)S(1)}, f32[2,1024,2]{2,1,0:T(8,128)S(1)}) custom-call(bf16[3,1024,256]{2,1,0:T(8,128)(2,1)S(1)} %qkv_forward.2.qkv_ref, f32[8,1]{1,0:T(8,128)S(1)} %copy.110.dep_ref), custom_call_target="tpu_custom_call" | custom-call | flops 12000000000 | bytes 4194304 | tf_op jit(solution)/shard_map/attend/pallas_call | solution.py:877
  98.8 6.0 %qkv_forward.3.dep_ref.qkv_ref = bf16[3,1024,256]{2,1,0:T(8,128)(2,1)S(1)} custom-call(bf16[4,128,1024]{2,1,0:T(8,128)(2,1)S(1)} %copy-done.15, bf16[4,128,1024]{2,1,0:T(8,128)(2,1)} %collective-permute-done.1.other_ref, bf16[1024,768]{1,0:T(8,128)(2,1)} %collective-permute-done.2.w_ref, bf16[256,256]{1,0:T(8,128)(2,1)S(1)} %copy-done.34, ...), custom_call_target="tpu_custom_call" | custom-call | flops 2684354560 | bytes 8388608 | tf_op jit(solution)/shard_map/qkv_forward/pallas_call | solution.py:406
  112.6 8.7 %attend.3 = (bf16[1024,256]{1,0:T(8,128)(2,1)S(1)}, f32[2,1024,2]{2,1,0:T(8,128)S(1)}) custom-call(bf16[3,1024,256]{2,1,0:T(8,128)(2,1)S(1)} %copy-done.27, bf16[4,128,1024]{2,1,0:T(8,128)(2,1)} %gated.1.dep_ref.gn_ref), custom_call_target="tpu_custom_call" | custom-call | flops 12000000000 | bytes 4194304 | tf_op jit(solution)/shard_map/attend/pallas_call | solution.py:877
  133.0 6.1 %all-to-all-start.4 = ((f32[8,1,8]{2,1,0:T(1,128)}), f32[8,1,8]{2,1,0:T(1,128)S(1)}, u32[]{:S(2)}, u32[]{:S(2)}) async-start(f32[8,1,8]{2,1,0:T(1,128)} %broadcast_in_dim.43), calls=%async_computation.4 | async-start | bytes 8192 | tf_op jit(solution)/shard_map/all_to_all | solution.py:1037
  139.8 5.7 %all-to-all-done.4 = f32[8,1,8]{2,1,0:T(1,128)S(1)} async-done(((f32[8,1,8]{2,1,0:T(1,128)}), f32[8,1,8]{2,1,0:T(1,128)S(1)}, u32[]{:S(2)}, u32[]{:S(2)}) %all-to-all-start.4) | async-done | bytes 288 | tf_op jit(solution)/shard_map/all_to_all | solution.py:1037
  145.8 5.7 %collective-permute-done.11.gn_ref = bf16[4,128,1024]{2,1,0:T(8,128)(2,1)} collective-permute-done((bf16[4,128,1024]{2,1,0:T(8,128)(2,1)}, bf16[4,128,1024]{2,1,0:T(8,128)(2,1)}, u32[]{:S(2)}, u32[]{:S(2)}) %collective-permute-start.11) | collective-permute-done | bytes 1048608 | tf_op jit(solution)/shard_map/ppermute | solution.py:1014
  152.6 16.2 %hidden.2 = (bf16[1024,1024]{1,0:T(8,128)(2,1)}, bf16[1024,1024]{1,0:T(8,128)(2,1)}, f32[4,128,1024]{2,1,0:T(8,128)}, bf16[4,128,1024]{2,1,0:T(8,128)(2,1)}, bf1...) custom-call(bf16[4,128,1024]{2,1,0:T(8,128)(2,1)} %get-tuple-element.54.near_ref, ...), custom_call_target="tpu_custom_call" | custom-call | flops 6442450944 | bytes 20971520 | tf_op jit(solution)/shard_map/hidden/pallas_call | solution.py:509
  169.3 3.9 fusion.17
  178.1 4.5 fusion.20
  182.6 4.4 fusion.19
  189.0 16.5 %hidden.3 = (bf16[1024,1024]{1,0:T(8,128)(2,1)}, bf16[1024,1024]{1,0:T(8,128)(2,1)}, f32[4,128,1024]{2,1,0:T(8,128)}, bf16[4,128,1024]{2,1,0:T(8,128)(2,1)}, bf1...) custom-call(bf16[4,128,1024]{2,1,0:T(8,128)(2,1)} %copy-done.72, ...), custom_call_target="tpu_custom_call" | custom-call | flops 6442450944 | bytes 20971520 | tf_op jit(solution)/shard_map/hidden/pallas_call | solution.py:509
  205.6 4.1 fusion.18
  213.5 3.9 add_convert_fusion.refs_9_
  220.0 3.9 add_convert_fusion.1.refs_8_
  227.2 16.9 %collective-permute-done.17.refs_2_ = bf16[4,128,1024]{2,1,0:T(8,128)(2,1)} collective-permute-done((bf16[4,128,1024]{2,1,0:T(8,128)(2,1)}, bf16[4,128,1024]{2,1,0:T(8,128)(2,1)}, u32[]{:S(2)}, u32[]{:S(2)}) %collective-permute-start.17) | collective-permute-done | bytes 1048608 | tf_op jit(solution)/shard_map/ppermute | solution.py:1014
  247.4 3.9 second_back.1
  272.4 14.8 %attend_back.2 = bf16[3,1024,256]{2,1,0:T(8,128)(2,1)S(1)} custom-call(bf16[3,1024,256]{2,1,0:T(8,128)(2,1)S(1)} %copy-done.28, bf16[1024,256]{1,0:T(8,128)(2,1)S(1)} %convolution_convert_fusion.3.grad_ref, f32[2,1024,2]{2,1,0:T(8,128)S(1)} %copy-done.40, f32[5,1024,128]{2,1,0:T(8,128)} %bitcast.150, ...), custom_call_target="tpu_custom_call" | custom-call | flops 24000000000 | bytes 6291456 | tf_op jit(solution)/shard_map/attend_back/pallas_call | solution.py:954
  293.6 5.2 %convolution_convert_fusion.refs_0_ = bf16[1024,768]{1,0:T(8,128)(2,1)} fusion(bf16[1024,1024]{1,0:T(8,128)(2,1)} %bitcast.163, bf16[1024,768]{0,1:T(8,128)(2,1)} %bitcast.156), kind=kOutput, calls=%fused_computation.16 | convolution fusion | flops 1611399168 | bytes 5242880 | tf_op jit(solution)/shard_map/dot_general | solution.py:1170
  299.6 4.0 last_gate.1
  303.7 14.8 %attend_back.3 = bf16[3,1024,256]{2,1,0:T(8,128)(2,1)S(1)} custom-call(bf16[3,1024,256]{2,1,0:T(8,128)(2,1)S(1)} %copy-done.38, bf16[1024,256]{1,0:T(8,128)(2,1)S(1)} %copy-done.36, f32[2,1024,2]{2,1,0:T(8,128)S(1)} %copy-done.42, f32[5,1024,128]{2,1,0:T(8,128)} %bitcast.151, bf16[1024,768]{1,0:T(8,128)(2,1)} %convolution_convert_fusion.refs_0_, ...), custom_call_target="tpu_custom_call" | custom-call | flops 24000000000 | bytes 6291456 | tf_op jit(solution)/shard_map/attend_back/pallas_call | solution.py:954
  330.2 5.8 %all-to-all-start.3 = ((bf16[8,64,1024]{2,1,0:T(8,128)(2,1)}), bf16[8,64,1024]{2,1,0:T(8,128)(2,1)}, u32[]{:S(2)}, u32[]{:S(2)}) async-start(bf16[8,64,1024]{2,1,0:T(8,128)(2,1)} %bitcast.22), calls=%async_computation.3 | async-start | bytes 2097152 | tf_op jit(solution)/shard_map/all_to_all | solution.py:1011
  343.6 5.7 %fusion.21.qkv_ref = f32[1024,768]{1,0:T(8,128)} fusion(bf16[1024,1024]{1,0:T(8,128)(2,1)} %bitcast.164, bf16[1024,768]{0,1:T(8,128)(2,1)} %bitcast.167), kind=kOutput, calls=%fused_computation.68 | convolution fusion | flops 1610612736 | bytes 6815744 | tf_op jit(solution)/shard_map/dot_general | solution.py:1170
  353.8 133.6 %depart.1 = (bf16[1024,768]{1,0:T(8,128)(2,1)}, bf16[256,1024]{1,0:T(8,128)(2,1)S(1)}, bf16[8,64,1024]{2,1,0:T(8,128)(2,1)S(1)}, bf16[16,48,256]{2,1,0:T(8,128)(2,1)S(1)}) custom-call(f32[1024,768]{1,0:T(8,128)} %fusion.21.qkv_ref, bf16[1024,768]{1,0:T(8,128)(2,1)} %collective-permute-done.19.qkv_far_ref, f32[256,1024]{1,0:T(8,128)S(1)} %copy-done.13, ...), custom_call_target="tpu_custom_call" | custom-call | tf_op jit(solution)/shard_map/depart/pallas_call | solution.py:810
  491.9 3.6 copy.133
  500.5 3.7 fusion.4
  504.3 4.2 convert_element_type.103
  (308 shorter events, 123.7 us)
Async XLA Ops:
  23.6 28.3 %all-to-all-start = ((bf16[8,64,1024]{2,1,0:T(8,128)(2,1)}), bf16[8,64,1024]{2,1,0:T(8,128)(2,1)S(1)}, u32[]{:S(2)}, u32[]{:S(2)}) async-start(bf16[8,64,1024]{2,1,0:T(8,128)(2,1)} %bitcast.168), calls=%async_computation | async-start | bytes 2097152 | tf_op jit(solution)/shard_map/all_to_all | solution.py:1011
  27.2 7.3 %collective-permute-start = (f32[4,2,6,256]{3,1,0,2:T(2,128)S(1)}, f32[4,2,6,256]{3,1,0,2:T(2,128)S(1)}, u32[]{:S(2)}, u32[]{:S(2)}) collective-permute-start(f32[4,2,6,256]{3,1,0,2:T(2,128)S(1)} %copy.103), channel_id=1, source_target_pairs={{0,1},{1,0},{2,3},{3,2},{4,5},{5,4},{6,7},{7,6},{8,9},{9,8},{10,11... | collective-permute-start | bytes 147464 | tf_op jit(solution)/shard_map/ppermute | solution.py:1017
  30.6 68.2 %collective-permute-start.2 = (bf16[1024,768]{1,0:T(8,128)(2,1)}, bf16[1024,768]{1,0:T(8,128)(2,1)}, u32[]{:S(2)}, u32[]{:S(2)}) collective-permute-start(bf16[1024,768]{1,0:T(8,128)(2,1)} %copy.109.w_ref), channel_id=1, source_target_pairs={{0,2},{1,3},{2,0},{3,1},{4,6},{5,7},{6,4},{7,5},{8,10},{9,11},{10,... | collective-permute-start | bytes 4718600 | tf_op jit(solution)/shard_map/ppermute | solution.py:1014
  32.5 50.1 %collective-permute-start.3 = (bf16[3,256]{1,0:T(4,128)(2,1)S(1)}, bf16[3,256]{1,0:T(4,128)(2,1)S(1)}, u32[]{:S(2)}, u32[]{:S(2)}) collective-permute-start(bf16[3,256]{1,0:T(4,128)(2,1)S(1)} %copy-done.69), channel_id=1, source_target_pairs={{0,2},{1,3},{2,0},{3,1},{4,6},{5,7},{6,4},{7,5},{8,10},{9,11},{10,... | collective-permute-start | bytes 4616 | tf_op jit(solution)/shard_map/ppermute | solution.py:1014
  32.7 88.6 %collective-permute-start.4 = (bf16[256,1024]{1,0:T(8,128)(2,1)}, bf16[256,1024]{1,0:T(8,128)(2,1)}, u32[]{:S(2)}, u32[]{:S(2)}) collective-permute-start(bf16[256,1024]{1,0:T(8,128)(2,1)} %w_ref.1), channel_id=1, source_target_pairs={{0,2},{1,3},{2,0},{3,1},{4,6},{5,7},{6,4},{7,5},{8,10},{9,11},{10,... | collective-permute-start | bytes 1572872 | tf_op jit(solution)/shard_map/ppermute | solution.py:1014
  52.0 54.8 %all-to-all-start.2 = ((bf16[8,64,1024]{2,1,0:T(8,128)(2,1)}), bf16[8,64,1024]{2,1,0:T(8,128)(2,1)S(1)}, u32[]{:S(2)}, u32[]{:S(2)}) async-start(bf16[8,64,1024]{2,1,0:T(8,128)(2,1)} %bitcast.169), calls=%async_computation.2 | async-start | bytes 2097152 | tf_op jit(solution)/shard_map/all_to_all | solution.py:1011
  57.0 26.3 %copy-start.14 = (bf16[4,128,1024]{2,1,0:T(8,128)(2,1)}, bf16[4,128,1024]{2,1,0:T(8,128)(2,1)S(1)}, u32[]{:S(2)}) copy-start(bf16[4,128,1024]{2,1,0:T(8,128)(2,1)S(1)} %first_norm.1.near_ref) | copy-start | bytes 3145732
  57.0 26.2 %collective-permute-start.1 = (bf16[4,128,1024]{2,1,0:T(8,128)(2,1)S(1)}, bf16[4,128,1024]{2,1,0:T(8,128)(2,1)}, u32[]{:S(2)}, u32[]{:S(2)}) collective-permute-start(bf16[4,128,1024]{2,1,0:T(8,128)(2,1)S(1)} %first_norm.1.near_ref), channel_id=1, source_target_pairs={{0,1},{1,0},{2,3},{3,2},{4,5},{5,4},{6,7},{7,6},{8,9},{9,8},{10,11... | collective-permute-start | bytes 3145736 | tf_op jit(solution)/shard_map/ppermute | solution.py:1017
  57.5 25.8 %copy-start.34 = (bf16[256,256]{1,0:T(8,128)(2,1)S(1)}, bf16[256,256]{1,0:T(8,128)(2,1)}, u32[]{:S(2)}) copy-start(bf16[256,256]{1,0:T(8,128)(2,1)} %constant.49.clone.swing_ref) | copy-start | bytes 393220
  124.5 2.7 collective-permute-start.5
  124.7 26.9 %collective-permute-start.7 = (bf16[4,128,1024]{2,1,0:T(8,128)(2,1)}, bf16[4,128,1024]{2,1,0:T(8,128)(2,1)}, u32[]{:S(2)}, u32[]{:S(2)}) collective-permute-start(bf16[4,128,1024]{2,1,0:T(8,128)(2,1)} %gated.1.dep_ref.gn_ref), channel_id=1, source_target_pairs={{0,1},{1,0},{2,3},{3,2},{4,5},{5,4},{6,7},{7,6},{8,9},{9,8},{10,11... | collective-permute-start | bytes 3145736 | tf_op jit(solution)/shard_map/ppermute | solution.py:1017
  125.3 26.3 %collective-permute-start.11 = (bf16[4,128,1024]{2,1,0:T(8,128)(2,1)}, bf16[4,128,1024]{2,1,0:T(8,128)(2,1)}, u32[]{:S(2)}, u32[]{:S(2)}) collective-permute-start(bf16[4,128,1024]{2,1,0:T(8,128)(2,1)} %gated.1.dep_ref.gn_ref), channel_id=1, source_target_pairs={{0,2},{1,3},{2,0},{3,1},{4,6},{5,7},{6,4},{7,5},{8,10},{9,11},{10,... | collective-permute-start | bytes 3145736 | tf_op jit(solution)/shard_map/ppermute | solution.py:1014
  132.3 19.3 %collective-permute-start.6 = (bf16[4,128,1024]{2,1,0:T(8,128)(2,1)}, bf16[4,128,1024]{2,1,0:T(8,128)(2,1)S(1)}, u32[]{:S(2)}, u32[]{:S(2)}) collective-permute-start(bf16[4,128,1024]{2,1,0:T(8,128)(2,1)} %get-tuple-element.54.near_ref), channel_id=1, source_target_pairs={{0,1},{1,0},{2,3},{3,2},{4,5},{5,4},{6,7},{7,6},{8,9},{9,8},{10,11... | collective-permute-start | bytes 3145736 | tf_op jit(solution)/shard_map/ppermute | solution.py:1017
  133.0 12.5 %all-to-all-start.4 = ((f32[8,1,8]{2,1,0:T(1,128)}), f32[8,1,8]{2,1,0:T(1,128)S(1)}, u32[]{:S(2)}, u32[]{:S(2)}) async-start(f32[8,1,8]{2,1,0:T(1,128)} %broadcast_in_dim.43), calls=%async_computation.4 | async-start | bytes 8192 | tf_op jit(solution)/shard_map/all_to_all | solution.py:1037
  145.8 23.6 %copy-start.70 = (bf16[1024,1024]{1,0:T(8,128)(2,1)S(1)}, bf16[1024,1024]{1,0:T(8,128)(2,1)}, u32[]{:S(2)}) copy-start(bf16[1024,1024]{1,0:T(8,128)(2,1)} %w2_ref.3) | copy-start | bytes 6291460
  145.8 30.6 %collective-permute-start.9 = (bf16[4,128,1024]{2,1,0:T(8,128)(2,1)}, bf16[4,128,1024]{2,1,0:T(8,128)(2,1)S(1)}, u32[]{:S(2)}, u32[]{:S(2)}) collective-permute-start(bf16[4,128,1024]{2,1,0:T(8,128)(2,1)} %get-tuple-element.54.near_ref), channel_id=1, source_target_pairs={{0,2},{1,3},{2,0},{3,1},{4,6},{5,7},{6,4},{7,5},{8,10},{9,11},{10,... | collective-permute-start | bytes 3145736 | tf_op jit(solution)/shard_map/ppermute | solution.py:1014
  151.6 35.4 %collective-permute-start.12 = (bf16[4,128,1024]{2,1,0:T(8,128)(2,1)}, bf16[4,128,1024]{2,1,0:T(8,128)(2,1)S(1)}, u32[]{:S(2)}, u32[]{:S(2)}) collective-permute-start(bf16[4,128,1024]{2,1,0:T(8,128)(2,1)} %collective-permute-done.11.gn_ref), channel_id=1, source_target_pairs={{0,1},{1,0},{2,3},{3,2},{4,5},{5,4},{6,7},{7,6},{8,9},{9,8},{10,11... | collective-permute-start | bytes 3145736 | tf_op jit(solution)/shard_map/ppermute | solution.py:1017
  168.8 58.4 %collective-permute-start.15 = (bf16[4,128,1024]{2,1,0:T(8,128)(2,1)}, bf16[4,128,1024]{2,1,0:T(8,128)(2,1)S(1)}, u32[]{:S(2)}, u32[]{:S(2)}) collective-permute-start(bf16[4,128,1024]{2,1,0:T(8,128)(2,1)} %get-tuple-element.59), channel_id=1, source_target_pairs={{0,1},{1,0},{2,3},{3,2},{4,5},{5,4},{6,7},{7,6},{8,9},{9,8},{10,11... | collective-permute-start | bytes 3145736 | tf_op jit(solution)/shard_map/ppermute | solution.py:1017
  176.4 10.6 %collective-permute-start.10 = (bf16[4,128,1024]{2,1,0:T(8,128)(2,1)S(1)}, bf16[4,128,1024]{2,1,0:T(8,128)(2,1)S(1)}, u32[]{:S(2)}, u32[]{:S(2)}) collective-permute-start(bf16[4,128,1024]{2,1,0:T(8,128)(2,1)S(1)} %collective-permute-done.9.near_ref), channel_id=1, source_target_pairs={{0,1},{1,0},{2,3},{3,2},{4,5},{5,4},{6,7},{7,6},{8,9},{9,8},{10,11... | collective-permute-start | bytes 3145736 | tf_op jit(solution)/shard_map/ppermute | solution.py:1017
  205.5 11.9 %collective-permute-start.16 = (bf16[4,128,1024]{2,1,0:T(8,128)(2,1)}, bf16[4,128,1024]{2,1,0:T(8,128)(2,1)S(1)}, u32[]{:S(2)}, u32[]{:S(2)}) collective-permute-start(bf16[4,128,1024]{2,1,0:T(8,128)(2,1)} %get-tuple-element.61), channel_id=1, source_target_pairs={{0,1},{1,0},{2,3},{3,2},{4,5},{5,4},{6,7},{7,6},{8,9},{9,8},{10,11... | collective-permute-start | bytes 3145736 | tf_op jit(solution)/shard_map/ppermute | solution.py:1017
  213.0 49.9 %collective-permute-start.13 = (bf16[4,128,1024]{2,1,0:T(8,128)(2,1)}, bf16[4,128,1024]{2,1,0:T(8,128)(2,1)}, u32[]{:S(2)}, u32[]{:S(2)}) collective-permute-start(bf16[4,128,1024]{2,1,0:T(8,128)(2,1)} %fusion.1), channel_id=1, source_target_pairs={{0,1},{1,0},{2,3},{3,2},{4,5},{5,4},{6,7},{7,6},{8,9},{9,8},{10,11... | collective-permute-start | bytes 3145736 | tf_op jit(solution)/shard_map/ppermute | solution.py:1017
  218.7 25.4 %collective-permute-start.17 = (bf16[4,128,1024]{2,1,0:T(8,128)(2,1)}, bf16[4,128,1024]{2,1,0:T(8,128)(2,1)}, u32[]{:S(2)}, u32[]{:S(2)}) collective-permute-start(bf16[4,128,1024]{2,1,0:T(8,128)(2,1)} %add_convert_fusion.2), channel_id=1, source_target_pairs={{0,2},{1,3},{2,0},{3,1},{4,6},{5,7},{6,4},{7,5},{8,10},{9,11},{10,... | collective-permute-start | bytes 3145736 | tf_op jit(solution)/shard_map/ppermute | solution.py:1014
  223.9 20.3 %copy-start.4 = (bf16[8,64,1024]{2,1,0:T(8,128)(2,1)S(1)}, bf16[8,64,1024]{2,1,0:T(8,128)(2,1)}, u32[]{:S(2)}) copy-start(bf16[8,64,1024]{2,1,0:T(8,128)(2,1)} %copy-done.3) | copy-start | bytes 3145732
  223.9 20.3 %copy-start.6 = (f32[4,128,1024]{2,1,0:T(8,128)S(1)}, f32[4,128,1024]{2,1,0:T(8,128)}, u32[]{:S(2)}) copy-start(f32[4,128,1024]{2,1,0:T(8,128)} %copy-done.5) | copy-start | bytes 6291460
  253.6 250.7 %all-reduce.5.cloned.1.call-start = ((), (), s32[]{:S(2)}) async-start(), calls=%async_computation.5 | async-start | bytes 8388608 | tf_op jit(solution)/shard_map/psum | solution.py:1116
  253.8 12.1 %collective-permute-start.18 = (bf16[4,128,1024]{2,1,0:T(8,128)(2,1)}, bf16[4,128,1024]{2,1,0:T(8,128)(2,1)}, u32[]{:S(2)}, u32[]{:S(2)}) collective-permute-start(bf16[4,128,1024]{2,1,0:T(8,128)(2,1)} %copy-done.30), channel_id=1, source_target_pairs={{0,1},{1,0},{2,3},{3,2},{4,5},{5,4},{6,7},{7,6},{8,9},{9,8},{10,11... | collective-permute-start | bytes 3145736 | tf_op jit(solution)/shard_map/ppermute | solution.py:1017
  262.4 37.2 %collective-permute-start.8 = (bf16[4,128,1024]{2,1,0:T(8,128)(2,1)}, bf16[4,128,1024]{2,1,0:T(8,128)(2,1)}, u32[]{:S(2)}, u32[]{:S(2)}) collective-permute-start(bf16[4,128,1024]{2,1,0:T(8,128)(2,1)} %fusion), channel_id=1, source_target_pairs={{0,1},{1,0},{2,3},{3,2},{4,5},{5,4},{6,7},{7,6},{8,9},{9,8},{10,11... | collective-permute-start | bytes 3145736 | tf_op jit(solution)/shard_map/ppermute | solution.py:1017
  265.5 34.1 %collective-permute-start.14 = (bf16[4,128,1024]{2,1,0:T(8,128)(2,1)}, bf16[4,128,1024]{2,1,0:T(8,128)(2,1)}, u32[]{:S(2)}, u32[]{:S(2)}) collective-permute-start(bf16[4,128,1024]{2,1,0:T(8,128)(2,1)} %add_convert_fusion.3), channel_id=1, source_target_pairs={{0,2},{1,3},{2,0},{3,1},{4,6},{5,7},{6,4},{7,5},{8,10},{9,11},{10,... | collective-permute-start | bytes 3145736 | tf_op jit(solution)/shard_map/ppermute | solution.py:1014
  298.8 55.0 %collective-permute-start.19 = (bf16[1024,768]{1,0:T(8,128)(2,1)}, bf16[1024,768]{1,0:T(8,128)(2,1)}, u32[]{:S(2)}, u32[]{:S(2)}) collective-permute-start(bf16[1024,768]{1,0:T(8,128)(2,1)} %convolution_convert_fusion.refs_0_), channel_id=1, source_target_pairs={{0,2},{1,3},{2,0},{3,1},{4,6},{5,7},{6,4},{7,5},{8,10},{9,11},{10,... | collective-permute-start | bytes 4718600 | tf_op jit(solution)/shard_map/ppermute | solution.py:1014
  329.1 20.3 %collective-permute-start.21 = (bf16[4,128,1024]{2,1,0:T(8,128)(2,1)}, bf16[4,128,1024]{2,1,0:T(8,128)(2,1)}, u32[]{:S(2)}, u32[]{:S(2)}) collective-permute-start(bf16[4,128,1024]{2,1,0:T(8,128)(2,1)} %fusion.2), channel_id=1, source_target_pairs={{0,1},{1,0},{2,3},{3,2},{4,5},{5,4},{6,7},{7,6},{8,9},{9,8},{10,11... | collective-permute-start | bytes 3145736 | tf_op jit(solution)/shard_map/ppermute | solution.py:1017
  329.1 24.7 %collective-permute-start.20 = (bf16[256,1024]{1,0:T(8,128)(2,1)}, bf16[256,1024]{1,0:T(8,128)(2,1)}, u32[]{:S(2)}, u32[]{:S(2)}) collective-permute-start(bf16[256,1024]{1,0:T(8,128)(2,1)} %convolution_convert_fusion.1), channel_id=1, source_target_pairs={{0,2},{1,3},{2,0},{3,1},{4,6},{5,7},{6,4},{7,5},{8,10},{9,11},{10,... | collective-permute-start | bytes 1572872 | tf_op jit(solution)/shard_map/ppermute | solution.py:1014
  330.2 174.0 %all-to-all-start.3 = ((bf16[8,64,1024]{2,1,0:T(8,128)(2,1)}), bf16[8,64,1024]{2,1,0:T(8,128)(2,1)}, u32[]{:S(2)}, u32[]{:S(2)}) async-start(bf16[8,64,1024]{2,1,0:T(8,128)(2,1)} %bitcast.22), calls=%async_computation.3 | async-start | bytes 2097152 | tf_op jit(solution)/shard_map/all_to_all | solution.py:1011
  (82 other events, 355.5 us)
Sparse Core Ops, SparseCore 0:
  265.9 219.4 all-reduce.4
